TPU v7x, 256 devices: a whole 4x4x8 slice. The times are simulated.
256 devices in a mesh: dp: 32 (over y, z), tensor: 8 (over x, core).
Axes of the slice: x: 4, y: 4, z: 8, core: 2. Of those that a mesh axis runs over, the one named last changes fastest.
Arguments:
- text_states: bfloat16 [32, 256, 4096], P('dp'), may hold values from -6 to 6
- prompt_lengths: int32 [32], P('dp'), may hold values from 1 to 256, as said below
- attn_gain: float32 [4096], replicated, may hold values from 0.1 to 1.9
- query_w: bfloat16 [4096, 2048], P('dp', 'tensor'), may hold values from -0.25 to 0.25
- key_w: bfloat16 [4096, 2048], P('dp', 'tensor'), may hold values from -0.25 to 0.25
- value_w: bfloat16 [4096, 2048], P('dp', 'tensor'), may hold values from -0.09375 to 0.09375
- out_w: bfloat16 [2048, 4096], P('tensor', 'dp'), may hold values from -0.125 to 0.125
- context_w: bfloat16 [4096, 2432], P('tensor', 'dp'), may hold values from -0.09375 to 0.09375
- mod_scale: float32 [32, 2432], P('dp'), may hold values from -0.5 to 0.5
- mod_shift: float32 [32, 2432], P('dp'), may hold values from -5 to 5
- text_key_w: bfloat16 [2432, 1536], P('dp', 'tensor'), may hold values from -0.125 to 0.125
- text_value_w: bfloat16 [2432, 1536], P('dp', 'tensor'), may hold values from -0.125 to 0.125
- image_query: bfloat16 [32, 512, 1536], P('dp', 'tensor'), may hold values from -30 to 30
- image_key: bfloat16 [32, 512, 1536], P('dp', 'tensor'), may hold values from -30 to 30
- image_value: bfloat16 [32, 512, 1536], P('dp', 'tensor'), may hold values from -6 to 6
Outputs:
- image_mixed: bfloat16 [32, 512, 1536], P('dp', 'tensor')
Inputs may be any that keep to these rules, and one draw needn't show every extreme that they name: `prompt_lengths`: some prompt has all 256 tokens in every draw.
All inputs are finite; a program needn't handle non-finite values.
Results may differ from a plain program's by a relative error of at most 0.015.
Values may be sent and summed in bfloat16 or wider, within the bound.
No kernel may reach another device: no remote copies, remote signals or barrier semaphores. Data moves between devices by JAX's collectives and lax.ppermute only.
A program may use at most 64 MiB of HBM per device.

v0:
```python
import jax
import jax.numpy as jnp
from jax import lax
from jax.sharding import PartitionSpec as P

HEAD = 64


EPS = 1e-06


def rms_scale(values, gain):
    return values * lax.rsqrt(jnp.mean(values * values, axis=-1, keepdims=True) + EPS) * gain


def masked_softmax(scores, valid):
    scores = jnp.where(valid, scores, -jnp.inf)
    top = jnp.max(scores, axis=-1, keepdims=True)
    expo = jnp.exp(scores - top)
    return (expo, jnp.sum(expo, axis=-1, keepdims=True))


def joint_sample(items):
    query, keys, values, text_keys, text_values, text_ok = items
    nheads = query.shape[-1] // HEAD
    all_keys = jnp.concatenate([keys, text_keys], axis=0).reshape(-1, nheads, HEAD)
    all_values = jnp.concatenate([values, text_values], axis=0).reshape(-1, nheads, HEAD)
    slot_ok = jnp.concatenate([lax.iota(jnp.int32, keys.shape[0]) >= 0, text_ok])
    scores = jnp.einsum(
        "qhd,khd->hqk",
        query.reshape(-1, nheads, HEAD),
        all_keys,
        preferred_element_type=jnp.float32,
    ) * HEAD ** (-0.5)
    expo, total = masked_softmax(scores, slot_ok[None, None, :])
    result = jnp.einsum(
        "hqk,khd->qhd", expo.astype(jnp.bfloat16), all_values, preferred_element_type=jnp.float32
    )
    result = result / jnp.swapaxes(total, 0, 1)
    return result.astype(jnp.bfloat16).reshape(query.shape[0], -1)


def per_device(
    text_states,
    prompt_lengths,
    attn_gain,
    query_w,
    key_w,
    value_w,
    out_w,
    context_w,
    mod_scale,
    mod_shift,
    text_key_w,
    text_value_w,
    image_query,
    image_key,
    image_value,
):
    prompts, slots, enc = text_states.shape
    flat = text_states.astype(jnp.float32).reshape(prompts * slots, enc)
    normed = rms_scale(flat, attn_gain).astype(jnp.bfloat16)
    local_width = query_w.shape[1]
    pieces = (
        lax.all_gather(query_w, "dp", axis=0, tiled=True),
        lax.all_gather(key_w, "dp", axis=0, tiled=True),
        lax.all_gather(value_w, "dp", axis=0, tiled=True),
    )
    columns = normed
    enc_q, enc_k, enc_v = tuple(
        (jnp.dot(columns, piece, preferred_element_type=jnp.float32) for piece in pieces)
    )
    heads_here = local_width // HEAD

    def split_heads(values):
        return values.astype(jnp.bfloat16).reshape(prompts, slots, heads_here, HEAD)

    enc_q = split_heads(enc_q)
    enc_k = split_heads(enc_k)
    enc_v = split_heads(enc_v)
    text_ok = lax.iota(jnp.int32, slots)[None, :] < prompt_lengths[:, None]
    scores = jnp.einsum("bqhd,bkhd->bhqk", enc_q, enc_k, preferred_element_type=jnp.float32)
    expo, total = masked_softmax(scores, text_ok[:, None, None, :])
    mixed = jnp.einsum(
        "bhqk,bkhd->bqhd", expo.astype(jnp.bfloat16), enc_v, preferred_element_type=jnp.float32
    )
    mixed = (
        (mixed / jnp.swapaxes(total, 1, 2))
        .astype(jnp.bfloat16)
        .reshape(prompts * slots, local_width)
    )
    partial_value = jnp.dot(
        mixed, lax.all_gather(out_w, "dp", axis=1, tiled=True), preferred_element_type=jnp.float32
    )
    share_width = context_w.shape[0]
    offset = lax.axis_index("tensor") * share_width
    summed = flat + lax.psum(partial_value.astype(jnp.bfloat16), "tensor").astype(jnp.float32)
    embedded = lax.dynamic_slice_in_dim(summed, offset, share_width, 1).astype(jnp.bfloat16)
    context_part = jnp.dot(
        embedded,
        lax.all_gather(context_w, "dp", axis=1, tiled=True),
        preferred_element_type=jnp.float32,
    )
    context = (
        lax.psum(context_part.astype(jnp.bfloat16), "tensor")
        .astype(jnp.float32)
        .reshape(prompts, slots, -1)
    )
    centered = context - jnp.mean(context, axis=-1, keepdims=True)
    spread = jnp.mean(centered * centered, axis=-1, keepdims=True)
    modulated = (
        centered * lax.rsqrt(spread + EPS) * (1.0 + mod_scale[:, None, :]) + mod_shift[:, None, :]
    )
    modulated = modulated.astype(jnp.bfloat16).reshape(prompts * slots, -1)
    text_width = text_key_w.shape[1]
    pieces = (
        lax.all_gather(text_key_w, "dp", axis=0, tiled=True),
        lax.all_gather(text_value_w, "dp", axis=0, tiled=True),
    )
    columns = modulated
    text_keys = jnp.dot(columns, pieces[0], preferred_element_type=jnp.float32)
    text_values = jnp.dot(columns, pieces[1], preferred_element_type=jnp.float32)
    text_keys = text_keys.astype(jnp.bfloat16).reshape(prompts, slots, text_width)
    text_values = text_values.astype(jnp.bfloat16).reshape(prompts, slots, text_width)
    by_head = (
        lax.all_to_all(image_query, "tensor", split_axis=2, concat_axis=1, tiled=True),
        lax.all_to_all(image_key, "tensor", split_axis=2, concat_axis=1, tiled=True),
        lax.all_to_all(image_value, "tensor", split_axis=2, concat_axis=1, tiled=True),
    )
    attended = lax.map(
        joint_sample, (by_head[0], by_head[1], by_head[2], text_keys, text_values, text_ok)
    )
    return lax.all_to_all(attended, "tensor", split_axis=1, concat_axis=2, tiled=True)


def solution(mesh):
    in_specs = (
        P("dp", None, None),
        P("dp"),
        P(),
        P("dp", "tensor"),
        P("dp", "tensor"),
        P("dp", "tensor"),
        P("tensor", "dp"),
        P("tensor", "dp"),
        P("dp", None),
        P("dp", None),
        P("dp", "tensor"),
        P("dp", "tensor"),
        P("dp", "tensor", None),
        P("dp", "tensor", None),
        P("dp", "tensor", None),
    )
    out_specs = P("dp", "tensor", None)
    return jax.shard_map(
        per_device, mesh=mesh, in_specs=in_specs, out_specs=out_specs, check_vma=False
    )
```

profile of v0, /device:TPU:1, one launch (start us, length us, event | category | flops | bytes accessed | tf_op | source)
XLA Modules:
  0.0 644.2 jit_solution(1232530552550823699)
XLA Ops:
  9.9 2.0 copy.60
  12.4 8.7 %reduce.11 = bf16[1536,64]{1,0:T(8,128)(2,1)S(1)} reduce(bf16[1536,1,64]{2,1,0:T(2,128)(2,1)S(1)} %bitcast.104, bf16[]{:T(256)} %broadcast.94), dimensions={1}, to_apply=%bitcast.81.reduce_sub_computation | reduce | bytes 393218
  22.1 6.5 %all-to-all-start.2 = ((bf16[8,2,6144]{2,1,0:T(2,128)(2,1)}), bf16[8,2,6144]{2,1,0:T(2,128)(2,1)S(1)}, u32[]{:S(2)}, u32[]{:S(2)}) async-start(bf16[8,2,6144]{2,1,0:T(2,128)(2,1)} %reshape.155), calls=%async_computation.2 | async-start | bytes 393216 | tf_op jit(solution)/shard_map/all_to_all | solution.py:126
  29.9 57.9 %all-gather.11.cloned.1.call-done = bf16[4096,256]{1,0:T(8,128)(2,1)} async-done(((bf16[128,256]{1,0:T(8,128)(2,1)}), bf16[4096,256]{1,0:T(8,128)(2,1)}) %all-gather.11.cloned.1.call-update) | async-done | bytes 2097168 | tf_op jit(solution)/shard_map/all_gather | solution.py:65
  87.8 2.7 convolution_convert_fusion.3
  90.5 75.0 %all-gather.13.cloned.1.call-done = bf16[4096,256]{1,0:T(8,128)(2,1)} async-done(((bf16[128,256]{1,0:T(8,128)(2,1)}), bf16[4096,256]{1,0:T(8,128)(2,1)}) %all-gather.13.cloned.1.call-update) | async-done | bytes 2097168 | tf_op jit(solution)/shard_map/all_gather | solution.py:66
  165.6 2.7 convolution_convert_fusion.2
  168.8 74.5 %all-gather.9.cloned.1.call-done = bf16[4096,256]{1,0:T(8,128)(2,1)} async-done(((bf16[128,256]{1,0:T(8,128)(2,1)}), bf16[4096,256]{1,0:T(8,128)(2,1)}) %all-gather.9.cloned.1.call-update) | async-done | bytes 2097168 | tf_op jit(solution)/shard_map/all_gather | solution.py:67
  243.3 2.7 convolution_convert_fusion.4
  246.4 72.1 %all-gather.15.cloned.1.call-done = bf16[256,4096]{1,0:T(8,128)(2,1)} async-done(((bf16[256,128]{1,0:T(8,128)(2,1)}), bf16[256,4096]{1,0:T(8,128)(2,1)}) %all-gather.15.cloned.1.call-update) | async-done | bytes 2097168 | tf_op jit(solution)/shard_map/all_gather | solution.py:93
  318.5 3.7 convolution_convert_fusion
  322.4 2.4 bitcast_convert_fusion
  324.8 73.9 %all-gather.17.cloned.1.call-done = bf16[32,76,512]{2,1,0:T(8,128)(2,1)} async-done(((bf16[1,76,512]{2,1,0:T(8,128)(2,1)}), bf16[32,76,512]{2,1,0:T(8,128)(2,1)}) %all-gather.17.cloned.1.call-update) | async-done | bytes 2490384 | tf_op jit(solution)/shard_map/all_gather | solution.py:101
  398.7 2.7 reshape.146
  401.4 68.9 %all-reduce.4.cloned.1.call-done = bf16[256,4096]{1,0:T(8,128)(2,1)} async-done(((bf16[256,4096]{1,0:T(8,128)(2,1)}), bf16[256,4096]{1,0:T(8,128)(2,1)}) %all-reduce.4.cloned.1.call-update) | async-done | bytes 2097168 | tf_op jit(solution)/shard_map/psum | solution.py:97
  470.3 3.0 convolution_convert_fusion.1
  473.9 8.7 %reduce.12 = bf16[1536,64]{1,0:T(8,128)(2,1)S(1)} reduce(bf16[1536,1,64]{2,1,0:T(2,128)(2,1)S(1)} %bitcast.108, bf16[]{:T(256)} %broadcast.94), dimensions={1}, to_apply=%bitcast.83.reduce_sub_computation | reduce | bytes 393218
  484.2 8.7 %reduce.13 = bf16[1536,64]{1,0:T(8,128)(2,1)S(1)} reduce(bf16[1536,1,64]{2,1,0:T(2,128)(2,1)S(1)} %bitcast.109, bf16[]{:T(256)} %broadcast.94), dimensions={1}, to_apply=%bitcast.85.reduce_sub_computation | reduce | bytes 393218
  492.9 1.0 reshape.159
  493.9 5.9 all-to-all-start.1
  499.8 41.4 %all-gather.2 = bf16[32,76,192]{2,1,0:T(8,128)(2,1)S(1)} all-gather(bf16[1,76,192]{2,1,0:T(8,128)(2,1)S(1)} %bitcast.123), channel_id=1, replica_groups=mesh['dp'=32,'tensor'=8] {'dp'}, dimensions={0}, use_global_device_ids=true | all-gather | bytes 963072 | tf_op jit(solution)/shard_map/all_gather | solution.py:117
  541.3 14.8 %all-to-all-start = ((bf16[8,2,6144]{2,1,0:T(2,128)(2,1)}), bf16[8,2,6144]{2,1,0:T(2,128)(2,1)S(1)}, u32[]{:S(2)}, u32[]{:S(2)}) async-start(bf16[8,2,6144]{2,1,0:T(2,128)(2,1)} %reshape.159), calls=%async_computation | async-start | bytes 393216 | tf_op jit(solution)/shard_map/all_to_all | solution.py:128
  556.1 37.9 %all-gather.1 = bf16[32,76,192]{2,1,0:T(8,128)(2,1)S(1)} all-gather(bf16[1,76,192]{2,1,0:T(8,128)(2,1)S(1)} %bitcast.124), channel_id=1, replica_groups=mesh['dp'=32,'tensor'=8] {'dp'}, dimensions={0}, use_global_device_ids=true | all-gather | bytes 963072 | tf_op jit(solution)/shard_map/all_gather | solution.py:118
  593.9 1.3 reshape.152
  595.3 1.3 reshape.151
  602.0 1.7 convert_reduce_fusion
  603.7 1.8 fusion.5
  607.4 1.1 bitcast_reduce_fusion
  608.5 1.0 fusion.1
  609.5 1.2 fusion.20
  611.1 2.2 reduce.14
  613.7 22.1 %all_to_all.63 = bf16[8,2,6144]{2,1,0:T(2,128)(2,1)S(1)} all-to-all(bf16[8,2,6144]{2,1,0:T(2,128)(2,1)S(1)} %reshape.161), channel_id=1, replica_groups=mesh['dp'=32,'tensor'=8] {'tensor'}, dimensions={0} | all-to-all | bytes 393216 | tf_op jit(solution)/shard_map/all_to_all | solution.py:133
  (80 shorter events, 17.8 us)
Async XLA Ops:
  6.5 22.8 %copy-start.1 = (bf16[1,256,4096]{2,1,0:T(8,128)(2,1)S(1)}, bf16[1,256,4096]{2,1,0:T(8,128)(2,1)}, u32[]{:S(2)}) copy-start(bf16[1,256,4096]{2,1,0:T(8,128)(2,1)} %param.15) | copy-start | bytes 6291460
  6.5 81.3 %all-gather.11.cloned.1.call-start = ((), (), s32[]{:S(2)}) async-start(), calls=%async_computation.5 | async-start | bytes 2162688 | tf_op jit(solution)/shard_map/all_gather | solution.py:65
  7.3 158.3 %all-gather.13.cloned.1.call-start = ((), (), s32[]{:S(2)}) async-start(), calls=%async_computation.6 | async-start | bytes 2162688 | tf_op jit(solution)/shard_map/all_gather | solution.py:66
  8.0 235.3 %all-gather.9.cloned.1.call-start = ((), (), s32[]{:S(2)}) async-start(), calls=%async_computation.4 | async-start | bytes 2162688 | tf_op jit(solution)/shard_map/all_gather | solution.py:67
  8.7 309.7 %all-gather.15.cloned.1.call-start = ((), (), s32[]{:S(2)}) async-start(), calls=%async_computation.7 | async-start | bytes 2162688 | tf_op jit(solution)/shard_map/all_gather | solution.py:93
  9.3 389.4 %all-gather.17.cloned.1.call-start = ((), (), s32[]{:S(2)}) async-start(), calls=%async_computation.10 | async-start | bytes 2703360 | tf_op jit(solution)/shard_map/all_gather | solution.py:101
  9.9 77.9 %copy-start.10 = (f32[4096]{0:T(1024)S(1)}, f32[4096]{0:T(1024)}, u32[]{:S(2)}) copy-start(f32[4096]{0:T(1024)} %param.17) | copy-start | bytes 49156
  22.1 471.8 %all-to-all-start.2 = ((bf16[8,2,6144]{2,1,0:T(2,128)(2,1)}), bf16[8,2,6144]{2,1,0:T(2,128)(2,1)S(1)}, u32[]{:S(2)}, u32[]{:S(2)}) async-start(bf16[8,2,6144]{2,1,0:T(2,128)(2,1)} %reshape.155), calls=%async_computation.2 | async-start | bytes 393216 | tf_op jit(solution)/shard_map/all_to_all | solution.py:126
  28.7 441.6 %all-reduce.4.cloned.1.call-start = ((), (), s32[]{:S(2)}) async-start(), calls=%async_computation.8 | async-start | bytes 4194304 | tf_op jit(solution)/shard_map/psum | solution.py:97
  322.2 279.7 %all-reduce.6.cloned.1.call-start = ((), (), s32[]{:S(2)}) async-start(), calls=%async_computation.9 | async-start | bytes 2490368 | tf_op jit(solution)/shard_map/psum | solution.py:105
  401.4 72.0 %copy-start.4 = (bf16[1,64,1536]{2,1,0:T(8,128)(2,1)S(1)}, bf16[1,64,1536]{2,1,0:T(8,128)(2,1)}, u32[]{:S(2)}) copy-start(bf16[1,64,1536]{2,1,0:T(8,128)(2,1)} %param.28) | copy-start | bytes 589828
  473.3 10.3 %copy-start.5 = (bf16[1,64,1536]{2,1,0:T(8,128)(2,1)S(1)}, bf16[1,64,1536]{2,1,0:T(8,128)(2,1)}, u32[]{:S(2)}) copy-start(bf16[1,64,1536]{2,1,0:T(8,128)(2,1)} %param.29) | copy-start | bytes 589828
  473.9 25.9 %copy-start.6 = (bf16[76,192]{1,0:T(8,128)(2,1)S(1)}, bf16[76,192]{1,0:T(8,128)(2,1)}, u32[]{:S(2)}) copy-start(bf16[76,192]{1,0:T(8,128)(2,1)} %param.25) | copy-start | bytes 87556
  483.7 72.4 %copy-start.7 = (bf16[76,192]{1,0:T(8,128)(2,1)S(1)}, bf16[76,192]{1,0:T(8,128)(2,1)}, u32[]{:S(2)}) copy-start(bf16[76,192]{1,0:T(8,128)(2,1)} %param.26) | copy-start | bytes 87556
  493.9 47.3 %all-to-all-start.1 = ((bf16[8,2,6144]{2,1,0:T(2,128)(2,1)}), bf16[8,2,6144]{2,1,0:T(2,128)(2,1)S(1)}, u32[]{:S(2)}, u32[]{:S(2)}) async-start(bf16[8,2,6144]{2,1,0:T(2,128)(2,1)} %reshape.157), calls=%async_computation.1 | async-start | bytes 393216 | tf_op jit(solution)/shard_map/all_to_all | solution.py:127
  541.3 58.9 %all-to-all-start = ((bf16[8,2,6144]{2,1,0:T(2,128)(2,1)}), bf16[8,2,6144]{2,1,0:T(2,128)(2,1)S(1)}, u32[]{:S(2)}, u32[]{:S(2)}) async-start(bf16[8,2,6144]{2,1,0:T(2,128)(2,1)} %reshape.159), calls=%async_computation | async-start | bytes 393216 | tf_op jit(solution)/shard_map/all_to_all | solution.py:128
  593.9 2.7 copy-start.8
  593.9 2.7 copy-start.9
  601.9 4.1 copy-start.2
  601.9 3.5 copy-start
  605.4 1.3 copy-start.3
Sparse Core Ops, SparseCore 0:
  9.9 77.8 all-gather.10
  90.4 75.1 all-gather.12
  168.2 75.1 all-gather.8
  245.7 72.7 all-gather.14
  320.9 77.7 all-gather.16
  400.9 69.3 all-reduce.3
  473.5 68.4 all-reduce.5
where the time goes:
time: 645 us; the launch traced here: 644 us
  waiting for transfers between devices  426 us (66%)
  blocking collectives  101 us (16%)
  other arithmetic  36.6 us (6%)
  starting transfers between devices  27.6 us (4%)
  local copies, waits for them, and re-layouts  19.3 us (3%)
  matrix products  19.1 us (3%)
  between operations  14.5 us (2%)
    all_gather x1, waiting for transfers between devices, per_device(): lax.all_gather(key_w, 'dp', axis=0, tiled=True)  75 us
    all_gather x1, waiting for transfers between devices, per_device(): lax.all_gather(value_w, 'dp', axis=0, tiled=True)  74.5 us
    all_gather x1, waiting for transfers between devices, per_device(): lax.all_gather(context_w, 'dp', axis=1, tiled=True)  73.9 us
    all_gather x1, waiting for transfers between devices, per_device(): lax.all_gather(out_w, 'dp', axis=1, tiled=True)  72.1 us
    psum x1, waiting for transfers between devices, per_device(): lax.psum(partial_value.astype(jnp.bfloat16), 'tensor').astype(jnp.float32)  68.9 us
    all_gather x1, waiting for transfers between devices, per_device(): lax.all_gather(query_w, 'dp', axis=0, tiled=True)  57.9 us
    all_gather x1, blocking collectives, per_device(): lax.all_gather(text_key_w, 'dp', axis=0, tiled=True)  41.4 us
    all_gather x1, blocking collectives, per_device(): lax.all_gather(text_value_w, 'dp', axis=0, tiled=True)  37.9 us
  transfers between devices with their start and end apart: 10, of which 6 were waited for; matrix products, arithmetic and copies ran while one was open for 9% of the time, Pallas kernels for 0%

commit v1 on v0

v1 whole, which is shorter than its diff:
```python
import jax
import jax.numpy as jnp
from jax import lax
from jax.sharding import Mesh
from jax.sharding import PartitionSpec as P

HEAD = 64
EPS = 1e-06
NY, NZ, NX, NC = 4, 8, 4, 2
DP = ("y", "z")
TENSOR = ("x", "c")
WIDTH = 2432
PIECE = 76
PADDED = 80
BF = jnp.bfloat16
F32 = jnp.float32


def shift(array, axis, size, step):
    return lax.ppermute(array, axis, [(i, (i + step) % size) for i in range(size)])


def ring_z(block):
    forward = backward = block
    found = [(0, block)]
    for step in range(1, 5):
        forward = shift(forward, "z", NZ, 1)
        found.append((-step, forward))
        if step < 4:
            backward = shift(backward, "z", NZ, -1)
            found.append((step, backward))
    return found


def share_y(block):
    return lax.all_to_all(
        jnp.broadcast_to(block[None], (NY,) + block.shape), "y", 0, 0, tiled=True
    )


def gather_z_first(shard):
    z = lax.axis_index("z")
    line = jnp.zeros((NZ,) + shard.shape, shard.dtype)
    for step, piece in ring_z(shard):
        line = lax.dynamic_update_slice_in_dim(line, piece[None], (z + step) % NZ, 0)
    return share_y(line)


def gather_y_first(shard):
    z = lax.axis_index("z")
    block = share_y(shard)
    plane = jnp.zeros((NY, NZ) + shard.shape, shard.dtype)
    for step, piece in ring_z(block):
        plane = lax.dynamic_update_slice_in_dim(plane, piece[:, None], (z + step) % NZ, 1)
    return plane


def lane_blocks(array):
    return [array[:, i : i + 128] for i in range(0, array.shape[1], 128)]


def masked_softmax(scores, valid):
    scores = jnp.where(valid, scores, -jnp.inf)
    top = jnp.max(scores, axis=-1, keepdims=True)
    expo = jnp.exp(scores - top)
    return (expo, jnp.sum(expo, axis=-1, keepdims=True))


def tensor_exchange(array):
    return lax.all_to_all(array, TENSOR, 0, 0, tiled=True)


def per_device(
    text_states,
    prompt_lengths,
    attn_gain,
    query_w,
    key_w,
    value_w,
    out_w,
    context_w,
    mod_scale,
    mod_shift,
    text_key_w,
    text_value_w,
    image_query,
    image_key,
    image_value,
):
    slots, enc = text_states.shape[1:]
    ndev = NX * NC
    me = lax.axis_index("x") * NC + lax.axis_index("c")
    pad_rows = ((0, PADDED - PIECE), (0, 0))
    context_t = jnp.pad(context_w.T, pad_rows)
    text_w = jnp.pad(jnp.concatenate([text_key_w, text_value_w], axis=1), pad_rows)
    packed = jnp.concatenate([out_w] + lane_blocks(context_t) + lane_blocks(text_w), axis=0)
    gathered = lax.all_gather(packed, DP, axis=0)

    qkv = jnp.concatenate([query_w, key_w, value_w], axis=1)
    half = qkv.shape[1] // 2
    w_b = gather_y_first(qkv[:, half:]).reshape(enc, half)
    w_a = gather_z_first(qkv[:, :half]).reshape(enc, half)

    flat = text_states[0].astype(F32)
    scale = lax.rsqrt(jnp.mean(flat * flat, axis=-1, keepdims=True) + EPS)
    normed = (flat * scale * attn_gain).astype(BF)

    nheads = image_query.shape[-1] // HEAD // ndev
    local = nheads * HEAD
    tokens = image_query.shape[1]
    image = jnp.concatenate(
        [
            jnp.swapaxes(part[0].reshape(tokens, ndev, local), 0, 1)
            for part in (image_query, image_key, image_value)
        ],
        axis=-1,
    )
    image = tensor_exchange(image).reshape(ndev * tokens, 3 * local)

    part_b = jnp.dot(normed, w_b, preferred_element_type=F32).astype(BF)
    part_a = jnp.dot(normed, w_a, preferred_element_type=F32).astype(BF)
    enc_all = jnp.concatenate([part_a, part_b], axis=1)
    width = query_w.shape[1]
    heads = width // HEAD
    enc_q, enc_k, enc_v = (
        enc_all[:, i * width : (i + 1) * width].reshape(slots, heads, HEAD) for i in range(3)
    )
    text_ok = lax.iota(jnp.int32, slots) < prompt_lengths[0]
    scores = jnp.einsum("qhd,khd->hqk", enc_q, enc_k, preferred_element_type=F32)
    expo, total = masked_softmax(scores, text_ok[None, None, :])
    mixed = jnp.einsum("hqk,khd->qhd", expo.astype(BF), enc_v, preferred_element_type=F32)
    mixed = (mixed / jnp.swapaxes(total, 0, 1)).astype(BF).reshape(slots, width)

    rows = out_w.shape[0]
    out_all = jnp.swapaxes(gathered[:, :rows], 0, 1).reshape(rows, enc)
    attn_part = jnp.dot(mixed, out_all, preferred_element_type=F32).astype(BF)
    share = enc // ndev
    attn_parts = tensor_exchange(jnp.swapaxes(attn_part.reshape(slots, ndev, share), 0, 1))
    attn = jnp.sum(attn_parts.astype(F32), axis=0)
    mine = lax.dynamic_slice_in_dim(text_states[0], me * share, share, 1)
    embedded = (mine.astype(F32) + attn).astype(BF)

    c_rows = PADDED * share // 128
    wide = NY * NZ * PADDED
    context_all = gathered[:, rows : rows + c_rows].reshape(NY * NZ, share // 128, PADDED, 128)
    context_all = jnp.swapaxes(context_all, 1, 2).reshape(wide, share)
    context_part = lax.dot_general(
        embedded, context_all, (((1,), (1,)), ((), ())), preferred_element_type=F32
    ).astype(BF)
    context = tensor_exchange(context_part.reshape(ndev, slots // ndev, wide))
    context = jnp.sum(context.astype(F32), axis=0)
    real = jnp.tile(lax.iota(jnp.int32, PADDED) < PIECE, NY * NZ)
    centered = jnp.where(real, context - jnp.sum(context, axis=-1, keepdims=True) / WIDTH, 0.0)
    spread = jnp.sum(centered * centered, axis=-1, keepdims=True) / WIDTH

    def spaced(row):
        return jnp.pad(row.reshape(NY * NZ, PIECE), ((0, 0), (0, PADDED - PIECE))).reshape(1, wide)

    modulated = centered * lax.rsqrt(spread + EPS) * (1.0 + spaced(mod_scale)) + spaced(mod_shift)
    modulated = modulated.astype(BF)
    modulated = tensor_exchange(jnp.broadcast_to(modulated[None], (ndev,) + modulated.shape))
    modulated = modulated.reshape(slots, wide)

    text_all = gathered[:, rows + c_rows :].reshape(NY * NZ, 2 * local // 128, PADDED, 128)
    text_all = jnp.swapaxes(text_all, 1, 2).reshape(wide, 2 * local)
    text_kv = jnp.dot(modulated, text_all, preferred_element_type=F32).astype(BF)

    def by_head(array):
        return array.reshape(array.shape[0], nheads, HEAD)

    query = by_head(image[:, :local])
    keys = by_head(jnp.concatenate([image[:, local : 2 * local], text_kv[:, :local]], axis=0))
    values = by_head(jnp.concatenate([image[:, 2 * local :], text_kv[:, local:]], axis=0))
    ok = jnp.concatenate([jnp.ones((ndev * tokens,), bool), text_ok])
    scores = jnp.einsum("qhd,khd->hqk", query, keys, preferred_element_type=F32) * HEAD ** (-0.5)
    expo, total = masked_softmax(scores, ok[None, None, :])
    result = jnp.einsum("hqk,khd->qhd", expo.astype(BF), values, preferred_element_type=F32)
    result = (result / jnp.swapaxes(total, 0, 1)).astype(BF).reshape(ndev, tokens, local)
    result = tensor_exchange(result)
    return jnp.swapaxes(result, 0, 1).reshape(1, tokens, ndev * local)


def solution(mesh):
    fine = Mesh(mesh.devices.reshape(NY, NZ, NX, NC), DP + TENSOR)
    in_specs = (
        P(DP, None, None),
        P(DP),
        P(),
        P(DP, TENSOR),
        P(DP, TENSOR),
        P(DP, TENSOR),
        P(TENSOR, DP),
        P(TENSOR, DP),
        P(DP, None),
        P(DP, None),
        P(DP, TENSOR),
        P(DP, TENSOR),
        P(DP, TENSOR, None),
        P(DP, TENSOR, None),
        P(DP, TENSOR, None),
    )
    out_specs = P(DP, TENSOR, None)
    return jax.shard_map(
        per_device, mesh=fine, in_specs=in_specs, out_specs=out_specs, check_vma=False
    )
```

time: 645 us -> 262 us (0.41)
  waiting for transfers between devices: 426 us -> 135 us
  blocking collectives: 101 us -> 9.76 us
  other arithmetic: 36.6 us -> 7.4 us
  starting transfers between devices: 27.6 us -> 48.2 us
  local copies, waits for them, and re-layouts: 19.3 us -> 31.7 us
    all_gather x5 -> x1, waiting for transfers between devices: 353 us -> 7.79 us  [per_device(): gathered = lax.all_gather(packed, DP, axis=0)]
    all_to_all x3 -> x6, waiting for transfers between devices: 0.01 us -> 80.1 us  [the longest x4 61.9 us: tensor_exchange(): return lax.all_to_all(array, TENSOR, 0, 0, tiled=True)]
    all_gather x2 -> x0, blocking collectives: 79.3 us -> none  [the longest x1 41.4 us: per_device(): lax.all_gather(text_key_w, 'dp', axis=0, tiled=True)]
    psum x2 -> x0, waiting for transfers between devices: 68.9 us -> none  [the longest x1 68.9 us: per_device(): lax.psum(partial_value.astype(jnp.bfloat16), 'tensor').astype(jnp.float32)]
    ppermute x0 -> x14, waiting for transfers between devices: none -> 47.5 us  [shift(): lax.ppermute(array, axis, [(i, (i + step) % size) for i in range(size)])]
    unnamed x5 -> x2, other arithmetic: 28.4 us -> 0.06 us
    ppermute x0 -> x14, starting transfers between devices: none -> 21.2 us  [shift(): lax.ppermute(array, axis, [(i, (i + step) % size) for i in range(size)])]
    all_to_all x1, blocking collectives: 22.1 us -> 9.76 us  [tensor_exchange(): return lax.all_to_all(array, TENSOR, 0, 0, tiled=True)]
  transfers between devices with their start and end apart: 10 -> 21, of which waited for: 6 -> 12; matrix products, arithmetic and copies ran while one was open for 9% -> 10% of each run, Pallas kernels for 0% -> 0%
where the time goes in v1:
time: 262 us; the launch traced here: 261 us
  waiting for transfers between devices  135 us (52%)
  starting transfers between devices  48.2 us (18%)
  local copies, waits for them, and re-layouts  31.7 us (12%)
  between operations  14.6 us (6%)
  matrix products  13.8 us (5%)
  blocking collectives  9.76 us (4%)
  other arithmetic  7.4 us (3%)
    all_to_all x4, waiting for transfers between devices, tensor_exchange(): return lax.all_to_all(array, TENSOR, 0, 0, tiled=True)  61.9 us
    ppermute x14, waiting for transfers between devices, shift(): lax.ppermute(array, axis, [(i, (i + step) % size) for i in range(size)])  47.5 us
    ppermute x14, starting transfers between devices, shift(): lax.ppermute(array, axis, [(i, (i + step) % size) for i in range(size)])  21.2 us
    all_to_all x4, starting transfers between devices, tensor_exchange(): return lax.all_to_all(array, TENSOR, 0, 0, tiled=True)  18.6 us
    all_to_all x2, waiting for transfers between devices, share_y(): lax.all_to_all(jnp.broadcast_to(block[None], (NY,) + block.shape), 'y', 0...  18.2 us
    all_to_all x1, blocking collectives, tensor_exchange(): return lax.all_to_all(array, TENSOR, 0, 0, tiled=True)  9.76 us
    all_to_all x2, starting transfers between devices, share_y(): lax.all_to_all(jnp.broadcast_to(block[None], (NY,) + block.shape), 'y', 0...  8.39 us
    all_gather x1, waiting for transfers between devices, per_device(): gathered = lax.all_gather(packed, DP, axis=0)  7.79 us
  transfers between devices with their start and end apart: 21, of which 12 were waited for; matrix products, arithmetic and copies ran while one was open for 10% of the time, Pallas kernels for 0%

profile of v1, /device:TPU:1, one launch (start us, length us, event | category | flops | bytes accessed | tf_op | source)
XLA Modules:
  0.0 260.9 jit_solution(10922672832098933192)
XLA Ops:
  13.8 2.5 collective-permute-start.7
  16.2 3.9 %collective-permute-start.8 = (bf16[128,384]{1,0:T(8,128)(2,1)}, bf16[128,384]{1,0:T(8,128)(2,1)S(1)}, u32[]{:S(2)}, u32[]{:S(2)}) collective-permute-start(bf16[128,384]{1,0:T(8,128)(2,1)} %get-tuple-element.8), channel_id=1, source_target_pairs={{0,56},{8,0},{16,8},{24,16},{32,24},{40,32},{48,40},{56,48},{1,57}... | collective-permute-start | bytes 294920 | tf_op jit(solution)/shard_map/ppermute | solution.py:20
  21.8 4.2 %all-to-all-start.1 = ((bf16[4,128,384]{2,1,0:T(8,128)(2,1)}), bf16[4,128,384]{2,1,0:T(8,128)(2,1)S(1)}, u32[]{:S(2)}, u32[]{:S(2)}) async-start(bf16[4,128,384]{2,1,0:T(8,128)(2,1)} %broadcast_in_dim.124), calls=%async_computation.1 | async-start | bytes 786432 | tf_op jit(solution)/shard_map/all_to_all | solution.py:36
  27.3 2.7 %collective-permute-start.10 = (bf16[128,384]{1,0:T(8,128)(2,1)S(1)}, bf16[128,384]{1,0:T(8,128)(2,1)S(1)}, u32[]{:S(2)}, u32[]{:S(2)}) collective-permute-start(bf16[128,384]{1,0:T(8,128)(2,1)S(1)} %collective-permute-done.8), channel_id=1, source_target_pairs={{0,56},{8,0},{16,8},{24,16},{32,24},{40,32},{48,40},{56,48},{1,57}... | collective-permute-start | bytes 294920 | tf_op jit(solution)/shard_map/ppermute | solution.py:20
  30.0 2.2 collective-permute-done.9
  32.3 3.2 %collective-permute-start.12 = (bf16[128,384]{1,0:T(8,128)(2,1)S(1)}, bf16[128,384]{1,0:T(8,128)(2,1)S(1)}, u32[]{:S(2)}, u32[]{:S(2)}) collective-permute-start(bf16[128,384]{1,0:T(8,128)(2,1)S(1)} %collective-permute-done.10), channel_id=1, source_target_pairs={{0,56},{8,0},{16,8},{24,16},{32,24},{40,32},{48,40},{56,48},{1,57}... | collective-permute-start | bytes 294920 | tf_op jit(solution)/shard_map/ppermute | solution.py:20
  35.6 2.7 %collective-permute-start.1 = (bf16[4,128,384]{2,1,0:T(8,128)(2,1)S(1)}, bf16[4,128,384]{2,1,0:T(8,128)(2,1)}, u32[]{:S(2)}, u32[]{:S(2)}) collective-permute-start(bf16[4,128,384]{2,1,0:T(8,128)(2,1)S(1)} %all-to-all-done.1), channel_id=1, source_target_pairs={{0,56},{8,0},{16,8},{24,16},{32,24},{40,32},{48,40},{56,48},{1,57}... | collective-permute-start | bytes 1179656 | tf_op jit(solution)/shard_map/ppermute | solution.py:20
  38.3 15.3 %collective-permute-done.13 = bf16[128,384]{1,0:T(8,128)(2,1)S(1)} collective-permute-done((bf16[128,384]{1,0:T(8,128)(2,1)S(1)}, bf16[128,384]{1,0:T(8,128)(2,1)S(1)}, u32[]{:S(2)}, u32[]{:S(2)}) %collective-permute-start.13) | collective-permute-done | bytes 98336 | tf_op jit(solution)/shard_map/ppermute | solution.py:20
  53.7 2.2 broadcast_in_dim.143
  55.9 4.2 %all-to-all-start.2 = ((bf16[4,8,128,384]{3,2,1,0:T(8,128)(2,1)}), bf16[4,8,128,384]{3,2,1,0:T(8,128)(2,1)S(1)}, u32[]{:S(2)}, u32[]{:S(2)}) async-start(bf16[4,8,128,384]{3,2,1,0:T(8,128)(2,1)} %broadcast_in_dim.143), calls=%async_computation.2 | async-start | bytes 6291456 | tf_op jit(solution)/shard_map/all_to_all | solution.py:36
  60.8 2.7 %collective-permute-start.3 = (bf16[4,128,384]{2,1,0:T(8,128)(2,1)}, bf16[4,128,384]{2,1,0:T(8,128)(2,1)S(1)}, u32[]{:S(2)}, u32[]{:S(2)}) collective-permute-start(bf16[4,128,384]{2,1,0:T(8,128)(2,1)} %collective-permute-done.1), channel_id=1, source_target_pairs={{0,56},{8,0},{16,8},{24,16},{32,24},{40,32},{48,40},{56,48},{1,57}... | collective-permute-start | bytes 1179656 | tf_op jit(solution)/shard_map/ppermute | solution.py:20
  65.6 4.6 %collective-permute-done.2 = bf16[4,128,384]{2,1,0:T(8,128)(2,1)S(1)} collective-permute-done((bf16[4,128,384]{2,1,0:T(8,128)(2,1)}, bf16[4,128,384]{2,1,0:T(8,128)(2,1)S(1)}, u32[]{:S(2)}, u32[]{:S(2)}) %collective-permute-start.2) | collective-permute-done | bytes 393248 | tf_op jit(solution)/shard_map/ppermute | solution.py:20
  70.9 3.4 %collective-permute-start.5 = (bf16[4,128,384]{2,1,0:T(8,128)(2,1)S(1)}, bf16[4,128,384]{2,1,0:T(8,128)(2,1)S(1)}, u32[]{:S(2)}, u32[]{:S(2)}) collective-permute-start(bf16[4,128,384]{2,1,0:T(8,128)(2,1)S(1)} %collective-permute-done.3), channel_id=1, source_target_pairs={{0,56},{8,0},{16,8},{24,16},{32,24},{40,32},{48,40},{56,48},{1,57}... | collective-permute-start | bytes 1179656 | tf_op jit(solution)/shard_map/ppermute | solution.py:20
  74.5 12.5 %collective-permute-done.4 = bf16[4,128,384]{2,1,0:T(8,128)(2,1)S(1)} collective-permute-done((bf16[4,128,384]{2,1,0:T(8,128)(2,1)S(1)}, bf16[4,128,384]{2,1,0:T(8,128)(2,1)S(1)}, u32[]{:S(2)}, u32[]{:S(2)}) %collective-permute-start.4) | collective-permute-done | bytes 393248 | tf_op jit(solution)/shard_map/ppermute | solution.py:20
  87.1 12.1 %collective-permute-done.6 = bf16[4,128,384]{2,1,0:T(8,128)(2,1)S(1)} collective-permute-done((bf16[4,128,384]{2,1,0:T(8,128)(2,1)S(1)}, bf16[4,128,384]{2,1,0:T(8,128)(2,1)S(1)}, u32[]{:S(2)}, u32[]{:S(2)}) %collective-permute-start.6) | collective-permute-done | bytes 393248 | tf_op jit(solution)/shard_map/ppermute | solution.py:20
  100.7 18.2 %all-to-all-done.2 = bf16[4,8,128,384]{3,2,1,0:T(8,128)(2,1)S(1)} async-done(((bf16[4,8,128,384]{3,2,1,0:T(8,128)(2,1)}), bf16[4,8,128,384]{3,2,1,0:T(8,128)(2,1)S(1)}, u32[]{:S(2)}, u32[]{:S(2)}) %all-to-all-start.2) | async-done | bytes 3145760 | tf_op jit(solution)/shard_map/all_to_all | solution.py:36
  118.9 2.9 %convolution_convert_fusion.2 = bf16[256,384]{1,0:T(8,128)(2,1)S(1)} fusion(bf16[4096,384]{1,0:T(8,128)(2,1)S(1)} %bitcast.158, bf16[1,256,4096]{2,1,0:T(8,128)(2,1)} %param.15, f32[4096]{0:T(1024)S(1)} %copy-done.9, f32[256]{0:T(256)S(1)} %add_rsqrt_fusion), kind=kOutput, calls=%fused_computation.28 | convolution fusion | flops 809598976 | bytes 5456896 | tf_op jit(solution)/shard_map/dot_general | solution.py:121
  123.0 7.8 %all-gather.3.cloned.1.call-done = bf16[26112,128]{1,0:T(8,128)(2,1)} async-done(((bf16[816,128]{1,0:T(8,128)(2,1)}), bf16[26112,128]{1,0:T(8,128)(2,1)}) %all-gather.3.cloned.1.call-update) | async-done | bytes 6684688 | tf_op jit(solution)/shard_map/all_gather | solution.py:97
  130.8 3.2 %slice_bitcast_fusion = bf16[256,32,128]{2,0,1:T(8,128)(2,1)} fusion(bf16[32,816,128]{2,1,0:T(8,128)(2,1)} %bitcast.154), kind=kLoop, calls=%fused_computation.21 | loop fusion | bytes 4194304 | tf_op jit(solution)/shard_map/transpose | solution.py:135
  134.0 3.3 %copy.108 = bf16[256,32,128]{0,2,1:T(8,128)(2,1)S(1)} copy(bf16[256,32,128]{2,0,1:T(8,128)(2,1)} %slice_bitcast_fusion) | data formatting | bytes 4194304 | tf_op jit(solution)/shard_map/transpose | solution.py:135
  139.5 4.7 %all-to-all-start.3 = ((bf16[8,256,512]{2,1,0:T(8,128)(2,1)}), bf16[8,256,512]{2,1,0:T(8,128)(2,1)S(1)}, u32[]{:S(2)}, u32[]{:S(2)}) async-start(bf16[8,256,512]{2,1,0:T(8,128)(2,1)} %bitcast.150), calls=%async_computation.3 | async-start | bytes 4194304 | tf_op jit(solution)/shard_map/all_to_all | solution.py:70
  146.2 2.9 %copy.110 = bf16[32,80,4,128]{3,2,1,0:T(4,128)(2,1)} copy(bf16[32,80,4,128]{3,1,2,0:T(8,128)(2,1)S(1)} %bitcast.149) | data formatting | bytes 5242880 | tf_op jit(solution)/shard_map/transpose | solution.py:146
  149.0 21.6 %all-to-all-done.3 = bf16[8,256,512]{2,1,0:T(8,128)(2,1)S(1)} async-done(((bf16[8,256,512]{2,1,0:T(8,128)(2,1)}), bf16[8,256,512]{2,1,0:T(8,128)(2,1)S(1)}, u32[]{:S(2)}, u32[]{:S(2)}) %all-to-all-start.3) | async-done | bytes 2097184 | tf_op jit(solution)/shard_map/all_to_all | solution.py:70
  170.9 3.8 %convolution_convert_fusion.1 = bf16[256,2560]{1,0:T(8,128)(2,1)} fusion(bf16[320,8,4,128]{3,2,1,0:T(4,128)(2,1)} %bitcast.160, f32[256,512]{1,0:T(8,128)S(1)} %convert_reduce_fusion, bf16[1,256,4096]{2,1,0:T(8,128)(2,1)} %param.15, s32[]{:T(128)S(6)} %select_n.102), kind=kOutput, calls=%fused_computation.10 | convolution fusion | flops 672137216 | bytes 4718596 | tf_op jit(solution)/shard_map/dot_general | solution.py:147
  174.8 4.5 %all-to-all-start.4 = ((bf16[8,32,2560]{2,1,0:T(8,128)(2,1)}), bf16[8,32,2560]{2,1,0:T(8,128)(2,1)S(1)}, u32[]{:S(2)}, u32[]{:S(2)}) async-start(bf16[8,32,2560]{2,1,0:T(8,128)(2,1)} %bitcast.48), calls=%async_computation.4 | async-start | bytes 2621440 | tf_op jit(solution)/shard_map/all_to_all | solution.py:70
  181.8 15.4 %all-to-all-done.4 = bf16[8,32,2560]{2,1,0:T(8,128)(2,1)S(1)} async-done(((bf16[8,32,2560]{2,1,0:T(8,128)(2,1)}), bf16[8,32,2560]{2,1,0:T(8,128)(2,1)S(1)}, u32[]{:S(2)}, u32[]{:S(2)}) %all-to-all-start.4) | async-done | bytes 1310752 | tf_op jit(solution)/shard_map/all_to_all | solution.py:70
  197.2 4.3 %all-to-all-start = ((bf16[8,64,576]{2,1,0:T(8,128)(2,1)}), bf16[8,64,576]{2,1,0:T(8,128)(2,1)S(1)}, u32[]{:S(2)}, u32[]{:S(2)}) async-start(bf16[8,64,576]{2,1,0:T(8,128)(2,1)} %pad_maximum_fusion), calls=%async_computation | async-start | bytes 1310720 | tf_op jit(solution)/shard_map/all_to_all | solution.py:70
  202.2 10.2 %all-to-all-done = bf16[8,64,576]{2,1,0:T(8,128)(2,1)S(1)} async-done(((bf16[8,64,576]{2,1,0:T(8,128)(2,1)}), bf16[8,64,576]{2,1,0:T(8,128)(2,1)S(1)}, u32[]{:S(2)}, u32[]{:S(2)}) %all-to-all-start) | async-done | bytes 589856 | tf_op jit(solution)/shard_map/all_to_all | solution.py:70
  213.7 5.0 %all-to-all-start.5 = ((bf16[8,32,2560]{2,1,0:T(8,128)(2,1)}), bf16[8,32,2560]{2,1,0:T(8,128)(2,1)}, u32[]{:S(2)}, u32[]{:S(2)}) async-start(bf16[8,32,2560]{2,1,0:T(8,128)(2,1)} %broadcast_in_dim.147), calls=%async_computation.5 | async-start | bytes 2621440 | tf_op jit(solution)/shard_map/all_to_all | solution.py:70
  222.0 14.8 %all-to-all-done.5 = bf16[8,32,2560]{2,1,0:T(8,128)(2,1)} async-done(((bf16[8,32,2560]{2,1,0:T(8,128)(2,1)}), bf16[8,32,2560]{2,1,0:T(8,128)(2,1)}, u32[]{:S(2)}, u32[]{:S(2)}) %all-to-all-start.5) | async-done | bytes 1310752 | tf_op jit(solution)/shard_map/all_to_all | solution.py:70
  236.7 2.2 fusion.18
  243.3 9.8 %all_to_all.35 = bf16[8,64,192]{2,1,0:T(8,128)(2,1)S(1)} all-to-all(bf16[8,64,192]{2,1,0:T(8,128)(2,1)S(1)} %copy.115), channel_id=1, replica_groups=mesh['y'=4,'z'=8,'x'=4,'c'=2] {'x','c'}, dimensions={0} | all-to-all | bytes 393216 | tf_op jit(solution)/shard_map/all_to_all | solution.py:70
  (123 shorter events, 33.5 us)
Async XLA Ops:
  6.5 20.1 %copy-start = (bf16[1,256,4096]{2,1,0:T(8,128)(2,1)S(1)}, bf16[1,256,4096]{2,1,0:T(8,128)(2,1)}, u32[]{:S(2)}) copy-start(bf16[1,256,4096]{2,1,0:T(8,128)(2,1)} %param.15) | copy-start | bytes 6291460
  6.5 124.2 %all-gather.3.cloned.1.call-start = ((), (), s32[]{:S(2)}) async-start(), calls=%async_computation.7 | async-start | bytes 6893568 | tf_op jit(solution)/shard_map/all_gather | solution.py:97
  11.4 0.7 copy-start.2
  13.8 13.4 %collective-permute-start.7 = (bf16[128,384]{1,0:T(8,128)(2,1)}, bf16[128,384]{1,0:T(8,128)(2,1)S(1)}, u32[]{:S(2)}, u32[]{:S(2)}) collective-permute-start(bf16[128,384]{1,0:T(8,128)(2,1)} %get-tuple-element.8), channel_id=1, source_target_pairs={{0,8},{8,16},{16,24},{24,32},{32,40},{40,48},{48,56},{56,0},{1,9},... | collective-permute-start | bytes 294920 | tf_op jit(solution)/shard_map/ppermute | solution.py:20
  16.2 11.1 %collective-permute-start.8 = (bf16[128,384]{1,0:T(8,128)(2,1)}, bf16[128,384]{1,0:T(8,128)(2,1)S(1)}, u32[]{:S(2)}, u32[]{:S(2)}) collective-permute-start(bf16[128,384]{1,0:T(8,128)(2,1)} %get-tuple-element.8), channel_id=1, source_target_pairs={{0,56},{8,0},{16,8},{24,16},{32,24},{40,32},{48,40},{56,48},{1,57}... | collective-permute-start | bytes 294920 | tf_op jit(solution)/shard_map/ppermute | solution.py:20
  21.8 13.7 %all-to-all-start.1 = ((bf16[4,128,384]{2,1,0:T(8,128)(2,1)}), bf16[4,128,384]{2,1,0:T(8,128)(2,1)S(1)}, u32[]{:S(2)}, u32[]{:S(2)}) async-start(bf16[4,128,384]{2,1,0:T(8,128)(2,1)} %broadcast_in_dim.124), calls=%async_computation.1 | async-start | bytes 786432 | tf_op jit(solution)/shard_map/all_to_all | solution.py:36
  27.2 5.1 %collective-permute-start.9 = (bf16[128,384]{1,0:T(8,128)(2,1)S(1)}, bf16[128,384]{1,0:T(8,128)(2,1)S(1)}, u32[]{:S(2)}, u32[]{:S(2)}) collective-permute-start(bf16[128,384]{1,0:T(8,128)(2,1)S(1)} %collective-permute-done.7), channel_id=1, source_target_pairs={{0,8},{8,16},{16,24},{24,32},{32,40},{40,48},{48,56},{56,0},{1,9},... | collective-permute-start | bytes 294920 | tf_op jit(solution)/shard_map/ppermute | solution.py:20
  27.3 5.0 %collective-permute-start.10 = (bf16[128,384]{1,0:T(8,128)(2,1)S(1)}, bf16[128,384]{1,0:T(8,128)(2,1)S(1)}, u32[]{:S(2)}, u32[]{:S(2)}) collective-permute-start(bf16[128,384]{1,0:T(8,128)(2,1)S(1)} %collective-permute-done.8), channel_id=1, source_target_pairs={{0,56},{8,0},{16,8},{24,16},{32,24},{40,32},{48,40},{56,48},{1,57}... | collective-permute-start | bytes 294920 | tf_op jit(solution)/shard_map/ppermute | solution.py:20
  32.3 6.0 %collective-permute-start.11 = (bf16[128,384]{1,0:T(8,128)(2,1)S(1)}, bf16[128,384]{1,0:T(8,128)(2,1)S(1)}, u32[]{:S(2)}, u32[]{:S(2)}) collective-permute-start(bf16[128,384]{1,0:T(8,128)(2,1)S(1)} %collective-permute-done.9), channel_id=1, source_target_pairs={{0,8},{8,16},{16,24},{24,32},{32,40},{40,48},{48,56},{56,0},{1,9},... | collective-permute-start | bytes 294920 | tf_op jit(solution)/shard_map/ppermute | solution.py:20
  32.3 6.0 %collective-permute-start.12 = (bf16[128,384]{1,0:T(8,128)(2,1)S(1)}, bf16[128,384]{1,0:T(8,128)(2,1)S(1)}, u32[]{:S(2)}, u32[]{:S(2)}) collective-permute-start(bf16[128,384]{1,0:T(8,128)(2,1)S(1)} %collective-permute-done.10), channel_id=1, source_target_pairs={{0,56},{8,0},{16,8},{24,16},{32,24},{40,32},{48,40},{56,48},{1,57}... | collective-permute-start | bytes 294920 | tf_op jit(solution)/shard_map/ppermute | solution.py:20
  35.5 25.2 %collective-permute-start = (bf16[4,128,384]{2,1,0:T(8,128)(2,1)S(1)}, bf16[4,128,384]{2,1,0:T(8,128)(2,1)}, u32[]{:S(2)}, u32[]{:S(2)}) collective-permute-start(bf16[4,128,384]{2,1,0:T(8,128)(2,1)S(1)} %all-to-all-done.1), channel_id=1, source_target_pairs={{0,8},{8,16},{16,24},{24,32},{32,40},{40,48},{48,56},{56,0},{1,9},... | collective-permute-start | bytes 1179656 | tf_op jit(solution)/shard_map/ppermute | solution.py:20
  35.6 25.2 %collective-permute-start.1 = (bf16[4,128,384]{2,1,0:T(8,128)(2,1)S(1)}, bf16[4,128,384]{2,1,0:T(8,128)(2,1)}, u32[]{:S(2)}, u32[]{:S(2)}) collective-permute-start(bf16[4,128,384]{2,1,0:T(8,128)(2,1)S(1)} %all-to-all-done.1), channel_id=1, source_target_pairs={{0,56},{8,0},{16,8},{24,16},{32,24},{40,32},{48,40},{56,48},{1,57}... | collective-permute-start | bytes 1179656 | tf_op jit(solution)/shard_map/ppermute | solution.py:20
  38.2 15.4 %collective-permute-start.13 = (bf16[128,384]{1,0:T(8,128)(2,1)S(1)}, bf16[128,384]{1,0:T(8,128)(2,1)S(1)}, u32[]{:S(2)}, u32[]{:S(2)}) collective-permute-start(bf16[128,384]{1,0:T(8,128)(2,1)S(1)} %collective-permute-done.11), channel_id=1, source_target_pairs={{0,8},{8,16},{16,24},{24,32},{32,40},{40,48},{48,56},{56,0},{1,9},... | collective-permute-start | bytes 294920 | tf_op jit(solution)/shard_map/ppermute | solution.py:20
  55.9 63.0 %all-to-all-start.2 = ((bf16[4,8,128,384]{3,2,1,0:T(8,128)(2,1)}), bf16[4,8,128,384]{3,2,1,0:T(8,128)(2,1)S(1)}, u32[]{:S(2)}, u32[]{:S(2)}) async-start(bf16[4,8,128,384]{3,2,1,0:T(8,128)(2,1)} %broadcast_in_dim.143), calls=%async_computation.2 | async-start | bytes 6291456 | tf_op jit(solution)/shard_map/all_to_all | solution.py:36
  60.6 38.7 %copy-start.1 = (bf16[1,256,4096]{2,1,0:T(8,128)(2,1)S(1)}, bf16[1,256,4096]{2,1,0:T(8,128)(2,1)}, u32[]{:S(2)}) copy-start(bf16[1,256,4096]{2,1,0:T(8,128)(2,1)} %param.15) | copy-start | bytes 6291460
  60.6 38.7 %copy-start.8 = (f32[4096]{0:T(1024)S(1)}, f32[4096]{0:T(1024)}, u32[]{:S(2)}) copy-start(f32[4096]{0:T(1024)} %param.17) | copy-start | bytes 49156
  60.7 9.5 %collective-permute-start.2 = (bf16[4,128,384]{2,1,0:T(8,128)(2,1)}, bf16[4,128,384]{2,1,0:T(8,128)(2,1)S(1)}, u32[]{:S(2)}, u32[]{:S(2)}) collective-permute-start(bf16[4,128,384]{2,1,0:T(8,128)(2,1)} %collective-permute-done), channel_id=1, source_target_pairs={{0,8},{8,16},{16,24},{24,32},{32,40},{40,48},{48,56},{56,0},{1,9},... | collective-permute-start | bytes 1179656 | tf_op jit(solution)/shard_map/ppermute | solution.py:20
  60.8 10.1 %collective-permute-start.3 = (bf16[4,128,384]{2,1,0:T(8,128)(2,1)}, bf16[4,128,384]{2,1,0:T(8,128)(2,1)S(1)}, u32[]{:S(2)}, u32[]{:S(2)}) collective-permute-start(bf16[4,128,384]{2,1,0:T(8,128)(2,1)} %collective-permute-done.1), channel_id=1, source_target_pairs={{0,56},{8,0},{16,8},{24,16},{32,24},{40,32},{48,40},{56,48},{1,57}... | collective-permute-start | bytes 1179656 | tf_op jit(solution)/shard_map/ppermute | solution.py:20
  70.2 16.8 %collective-permute-start.4 = (bf16[4,128,384]{2,1,0:T(8,128)(2,1)S(1)}, bf16[4,128,384]{2,1,0:T(8,128)(2,1)S(1)}, u32[]{:S(2)}, u32[]{:S(2)}) collective-permute-start(bf16[4,128,384]{2,1,0:T(8,128)(2,1)S(1)} %collective-permute-done.2), channel_id=1, source_target_pairs={{0,8},{8,16},{16,24},{24,32},{32,40},{40,48},{48,56},{56,0},{1,9},... | collective-permute-start | bytes 1179656 | tf_op jit(solution)/shard_map/ppermute | solution.py:20
  70.9 16.1 %collective-permute-start.5 = (bf16[4,128,384]{2,1,0:T(8,128)(2,1)S(1)}, bf16[4,128,384]{2,1,0:T(8,128)(2,1)S(1)}, u32[]{:S(2)}, u32[]{:S(2)}) collective-permute-start(bf16[4,128,384]{2,1,0:T(8,128)(2,1)S(1)} %collective-permute-done.3), channel_id=1, source_target_pairs={{0,56},{8,0},{16,8},{24,16},{32,24},{40,32},{48,40},{56,48},{1,57}... | collective-permute-start | bytes 1179656 | tf_op jit(solution)/shard_map/ppermute | solution.py:20
  87.0 12.3 %collective-permute-start.6 = (bf16[4,128,384]{2,1,0:T(8,128)(2,1)S(1)}, bf16[4,128,384]{2,1,0:T(8,128)(2,1)S(1)}, u32[]{:S(2)}, u32[]{:S(2)}) collective-permute-start(bf16[4,128,384]{2,1,0:T(8,128)(2,1)S(1)} %collective-permute-done.4), channel_id=1, source_target_pairs={{0,8},{8,16},{16,24},{24,32},{32,40},{40,48},{48,56},{56,0},{1,9},... | collective-permute-start | bytes 1179656 | tf_op jit(solution)/shard_map/ppermute | solution.py:20
  99.3 19.6 %copy-start.9 = (f32[4096]{0:T(1024)S(1)}, f32[4096]{0:T(1024)}, u32[]{:S(2)}) copy-start(f32[4096]{0:T(1024)} %param.17) | copy-start | bytes 49156
  139.5 31.1 %all-to-all-start.3 = ((bf16[8,256,512]{2,1,0:T(8,128)(2,1)}), bf16[8,256,512]{2,1,0:T(8,128)(2,1)S(1)}, u32[]{:S(2)}, u32[]{:S(2)}) async-start(bf16[8,256,512]{2,1,0:T(8,128)(2,1)} %bitcast.150), calls=%async_computation.3 | async-start | bytes 4194304 | tf_op jit(solution)/shard_map/all_to_all | solution.py:70
  170.9 8.5 %copy-start.6 = (f32[1,2432]{1,0:T(1,128)S(1)}, f32[1,2432]{1,0:T(1,128)}, u32[]{:S(2)}) copy-start(f32[1,2432]{1,0:T(1,128)} %param.23) | copy-start | bytes 29188
  170.9 8.7 %copy-start.7 = (f32[1,2432]{1,0:T(1,128)S(1)}, f32[1,2432]{1,0:T(1,128)}, u32[]{:S(2)}) copy-start(f32[1,2432]{1,0:T(1,128)} %param.24) | copy-start | bytes 29188
  170.9 8.9 %copy-start.3 = (bf16[1,64,1536]{2,1,0:T(8,128)(2,1)S(1)}, bf16[1,64,1536]{2,1,0:T(8,128)(2,1)}, u32[]{:S(2)}) copy-start(bf16[1,64,1536]{2,1,0:T(8,128)(2,1)} %param.29) | copy-start | bytes 589828
  174.8 5.3 %copy-start.4 = (bf16[1,64,1536]{2,1,0:T(8,128)(2,1)S(1)}, bf16[1,64,1536]{2,1,0:T(8,128)(2,1)}, u32[]{:S(2)}) copy-start(bf16[1,64,1536]{2,1,0:T(8,128)(2,1)} %param.28) | copy-start | bytes 589828
  174.8 5.6 %copy-start.5 = (bf16[1,64,1536]{2,1,0:T(8,128)(2,1)S(1)}, bf16[1,64,1536]{2,1,0:T(8,128)(2,1)}, u32[]{:S(2)}) copy-start(bf16[1,64,1536]{2,1,0:T(8,128)(2,1)} %param.27) | copy-start | bytes 589828
  174.8 22.4 %all-to-all-start.4 = ((bf16[8,32,2560]{2,1,0:T(8,128)(2,1)}), bf16[8,32,2560]{2,1,0:T(8,128)(2,1)S(1)}, u32[]{:S(2)}, u32[]{:S(2)}) async-start(bf16[8,32,2560]{2,1,0:T(8,128)(2,1)} %bitcast.48), calls=%async_computation.4 | async-start | bytes 2621440 | tf_op jit(solution)/shard_map/all_to_all | solution.py:70
  197.2 15.2 %all-to-all-start = ((bf16[8,64,576]{2,1,0:T(8,128)(2,1)}), bf16[8,64,576]{2,1,0:T(8,128)(2,1)S(1)}, u32[]{:S(2)}, u32[]{:S(2)}) async-start(bf16[8,64,576]{2,1,0:T(8,128)(2,1)} %pad_maximum_fusion), calls=%async_computation | async-start | bytes 1310720 | tf_op jit(solution)/shard_map/all_to_all | solution.py:70
  213.7 23.1 %all-to-all-start.5 = ((bf16[8,32,2560]{2,1,0:T(8,128)(2,1)}), bf16[8,32,2560]{2,1,0:T(8,128)(2,1)}, u32[]{:S(2)}, u32[]{:S(2)}) async-start(bf16[8,32,2560]{2,1,0:T(8,128)(2,1)} %broadcast_in_dim.147), calls=%async_computation.5 | async-start | bytes 2621440 | tf_op jit(solution)/shard_map/all_to_all | solution.py:70
Sparse Core Ops, SparseCore 0:
  12.2 118.4 all-gather.2

commit v2 on v1

v2 whole, which is shorter than its diff:
```python
import functools

import jax
import jax.numpy as jnp
from jax import lax
from jax.experimental import pallas as pl
from jax.experimental.pallas import tpu as pltpu
from jax.sharding import Mesh
from jax.sharding import PartitionSpec as P

HEAD = 64
EPS = 1e-06
NY, NZ, NX, NC = 4, 8, 4, 2
DP = ("y", "z")
TENSOR = ("x", "c")
WIDTH = 2432
PIECE = 76
PADDED = 80
BF = jnp.bfloat16
F32 = jnp.float32


def shift(array, axis, size, step):
    return lax.ppermute(array, axis, [(i, (i + step) % size) for i in range(size)])


def gather_weights(shard, later):
    half = shard.shape[0] // 2
    y = lax.axis_index("y")

    def z_pair(ahead, behind):
        return shift(ahead, "z", NZ, 1), shift(behind, "z", NZ, -1)

    up, down = shift(shard, "y", NY, 1), shift(shard, "y", NY, -1)
    far = [shift(up[:half], "y", NY, 1), shift(down[half:], "y", NY, -1)]
    far = jnp.concatenate(far, axis=0)
    block = jnp.zeros((NY,) + shard.shape, shard.dtype)
    for step, piece in ((0, shard), (-1, up), (1, down), (2, far)):
        block = lax.dynamic_update_slice_in_dim(block, piece[None], (y + step) % NY, 0)
    block, *later = lax.optimization_barrier((block, *later))
    s1, t1 = z_pair(block, block)
    s2, t2 = z_pair(s1, t1)
    s3, t3 = z_pair(s2, t2)
    s4 = shift(s3[: NY // 2], "z", NZ, 1)
    t4 = shift(t3[NY // 2 :], "z", NZ, -1)
    last = jnp.concatenate([s4, t4], axis=0)
    ring = [(0, block), (-1, s1), (1, t1), (-2, s2), (2, t2), (-3, s3), (3, t3), (4, last)]
    return ring, later


def encoder_kernel(
    heads, steps, length_ref, states_ref, qk_w_ref, v_ref, out_w_ref, out_ref, qk_ref, mixed_ref
):
    i = pl.program_id(0)
    width = heads * HEAD
    depth = qk_w_ref.shape[2]

    @pl.when(i == 0)
    def _():
        qk_ref[...] = jnp.zeros_like(qk_ref)

    @pl.when(i < steps)
    def _():
        weights = [
            jnp.concatenate([qk_w_ref[k, n : n + depth] for n in range(0, 2 * width, depth)], axis=1)
            for k in range(qk_w_ref.shape[0])
        ]
        qk_ref[...] += jnp.dot(
            states_ref[...], jnp.concatenate(weights, axis=0), preferred_element_type=F32
        )

    @pl.when(i == steps - 1)
    def _():
        slots = qk_ref.shape[0]
        ok = lax.broadcasted_iota(jnp.int32, (slots, slots), 1) < length_ref[0]
        for h in range(heads):
            cols = slice(h * HEAD, (h + 1) * HEAD)
            query = qk_ref[:, cols].astype(BF)
            key = qk_ref[:, width + h * HEAD : width + (h + 1) * HEAD].astype(BF)
            scores = lax.dot_general(
                query, key, (((1,), (1,)), ((), ())), preferred_element_type=F32
            )
            scores = jnp.where(ok, scores, -jnp.inf)
            expo = jnp.exp(scores - jnp.max(scores, axis=-1, keepdims=True))
            total = jnp.sum(expo, axis=-1, keepdims=True)
            mixed = jnp.dot(expo.astype(BF), v_ref[:, cols], preferred_element_type=F32)
            mixed_ref[:, cols] = (mixed / total).astype(BF)

    @pl.when(i >= steps)
    def _():
        for k in range(out_ref.shape[0]):
            out_ref[k] = jnp.dot(
                mixed_ref[...], out_w_ref[k], preferred_element_type=F32
            ).astype(BF)


def encoder(length, states, gathered, row, v, w_out):
    slots, width = v.shape
    pieces, rows, cols = w_out.shape
    shard = states.shape[1] // pieces
    at_once, steps = 4, pieces // 4
    out_at_once = 8

    def early(i):
        return jnp.minimum(i, steps - 1)

    def late(i):
        return jnp.maximum(i - steps, 0)

    return pl.pallas_call(
        functools.partial(encoder_kernel, width // HEAD, steps),
        grid=(steps + pieces // out_at_once,),
        in_specs=[
            pl.BlockSpec(memory_space=pltpu.SMEM),
            pl.BlockSpec((slots, at_once * shard), lambda i: (0, early(i))),
            pl.BlockSpec(
                (pl.Element(at_once), pl.Element(2 * width // 128 * shard), pl.Element(128)),
                lambda i: (early(i) * at_once, row, 0),
            ),
            pl.BlockSpec(v.shape, lambda i: (0, 0)),
            pl.BlockSpec((out_at_once, rows, cols), lambda i: (late(i), 0, 0)),
        ],
        out_specs=pl.BlockSpec((out_at_once, slots, cols), lambda i: (late(i), 0, 0)),
        out_shape=jax.ShapeDtypeStruct((pieces, slots, cols), BF),
        scratch_shapes=[pltpu.VMEM((slots, 2 * width), F32), pltpu.VMEM((slots, width), BF)],
        compiler_params=pltpu.CompilerParams(vmem_limit_bytes=40 * 2**20),
        cost_estimate=pl.CostEstimate(
            flops=2 * slots * (rows * pieces * cols + 2 * width * pieces * shard),
            bytes_accessed=pieces * 2 * (cols * (rows + slots) + shard * (slots + 2 * width)),
            transcendentals=slots * slots * width // HEAD,
        ),
    )(length, states, gathered, v, w_out)


def context_kernel(embedded_ref, weights_ref, out_ref):
    for k in range(weights_ref.shape[0]):
        total = 0
        for n in range(embedded_ref.shape[0]):
            total += lax.dot_general(
                weights_ref[k, n * PADDED : (n + 1) * PADDED],
                embedded_ref[n],
                (((1,), (1,)), ((), ())),
                preferred_element_type=F32,
            )
        out_ref[k] = total.astype(BF)


def embed_context(embedded, gathered, row):
    blocks, slots, _ = embedded.shape
    pieces = gathered.shape[0]
    at_once = 8
    return pl.pallas_call(
        context_kernel,
        grid=(pieces // at_once,),
        in_specs=[
            pl.BlockSpec(embedded.shape, lambda i: (0, 0, 0)),
            pl.BlockSpec(
                (pl.Element(at_once), pl.Element(blocks * PADDED), pl.Element(128)),
                lambda i: (i * at_once, row, 0),
            ),
        ],
        out_specs=pl.BlockSpec((at_once, PADDED, slots), lambda i: (i, 0, 0)),
        out_shape=jax.ShapeDtypeStruct((pieces, PADDED, slots), BF),
        compiler_params=pltpu.CompilerParams(vmem_limit_bytes=40 * 2**20),
        cost_estimate=pl.CostEstimate(
            flops=2 * pieces * PADDED * blocks * 128 * slots,
            bytes_accessed=pieces * PADDED * 2 * (blocks * 128 + slots),
            transcendentals=0,
        ),
    )(embedded, gathered)


def joint_kernel(
    row, length_ref, context_ref, scale_ref, shift_ref, image_ref, gathered_ref, out_ref, text_ref, sem
):
    pieces, rows, slots = context_ref.shape
    cols = text_ref.shape[1] // rows
    local = out_ref.shape[1]
    copy = pltpu.make_async_copy(
        gathered_ref.at[:, pl.ds(row, cols * rows)], text_ref, sem.at[0]
    )
    copy.start()
    real = lax.broadcasted_iota(jnp.int32, (rows, slots), 0) < PIECE
    total = jnp.zeros((rows, slots), F32)
    for k in range(pieces):
        total += context_ref[k].astype(F32)
    mean = jnp.sum(total, axis=0, keepdims=True) / WIDTH
    square = jnp.zeros((rows, slots), F32)
    for k in range(pieces):
        centered = context_ref[k].astype(F32) - mean
        square += centered * centered
    square = jnp.where(real, square, 0.0)
    factor = lax.rsqrt(jnp.sum(square, axis=0, keepdims=True) / WIDTH + EPS)
    copy.wait()
    text = jnp.zeros((cols * 128, slots), F32)
    for k in range(pieces):
        scale = 1.0 + jnp.concatenate([scale_ref[k]] * (slots // 128), axis=1)
        move = jnp.concatenate([shift_ref[k]] * (slots // 128), axis=1)
        modulated = (context_ref[k].astype(F32) - mean) * factor * scale + move
        modulated = jnp.where(real, modulated, 0.0).astype(BF)
        weights = [text_ref[k, n * rows : (n + 1) * rows] for n in range(cols)]
        text += lax.dot_general(
            jnp.concatenate(weights, axis=1),
            modulated,
            (((0,), (0,)), ((), ())),
            preferred_element_type=F32,
        )
    text = text.astype(BF)
    tokens = image_ref.shape[0]
    ok = lax.broadcasted_iota(jnp.int32, (tokens, slots), 1) < length_ref[0]
    for h in range(local // HEAD):
        at = h * HEAD
        query = image_ref[:, at : at + HEAD]
        key = image_ref[:, local + at : local + at + HEAD]
        value = image_ref[:, 2 * local + at : 2 * local + at + HEAD]
        near = lax.dot_general(query, key, (((1,), (1,)), ((), ())), preferred_element_type=F32)
        near = near * HEAD ** (-0.5)
        far = jnp.dot(query, text[at : at + HEAD], preferred_element_type=F32) * HEAD ** (-0.5)
        far = jnp.where(ok, far, -jnp.inf)
        top = jnp.maximum(
            jnp.max(near, axis=-1, keepdims=True), jnp.max(far, axis=-1, keepdims=True)
        )
        near, far = jnp.exp(near - top), jnp.exp(far - top)
        sums = jnp.sum(near, axis=-1, keepdims=True) + jnp.sum(far, axis=-1, keepdims=True)
        result = jnp.dot(near.astype(BF), value, preferred_element_type=F32)
        result += lax.dot_general(
            far.astype(BF),
            text[local + at : local + at + HEAD],
            (((1,), (1,)), ((), ())),
            preferred_element_type=F32,
        )
        out_ref[:, at : at + HEAD] = (result / sums).astype(BF)


def joint(length, context, scale, move, image, gathered, row):
    pieces, rows, slots = context.shape
    tokens, cols = image.shape
    text_rows = gathered.shape[1] - row
    vmem = pl.BlockSpec(memory_space=pltpu.VMEM)
    return pl.pallas_call(
        functools.partial(joint_kernel, row),
        in_specs=[pl.BlockSpec(memory_space=pltpu.SMEM)]
        + [vmem] * 4
        + [pl.BlockSpec(memory_space=pl.ANY)],
        out_specs=vmem,
        out_shape=jax.ShapeDtypeStruct((tokens, cols // 3), BF),
        scratch_shapes=[
            pltpu.VMEM((pieces, text_rows, 128), BF),
            pltpu.SemaphoreType.DMA((1,)),
        ],
        compiler_params=pltpu.CompilerParams(vmem_limit_bytes=48 * 2**20),
        cost_estimate=pl.CostEstimate(
            flops=2 * pieces * rows * text_rows // rows * 128 * slots
            + 4 * tokens * (tokens + slots) * cols // 3,
            bytes_accessed=pieces * rows * 2 * (slots + text_rows // rows * 128),
            transcendentals=tokens * (tokens + slots) * cols // 3 // HEAD,
        ),
    )(length, context, scale, move, image, gathered)


def lane_blocks(array):
    return [array[:, i : i + 128] for i in range(0, array.shape[1], 128)]


def tensor_exchange(array):
    return lax.all_to_all(array, TENSOR, 0, 0, tiled=True)


def take(array, index, axis=0):
    return lax.dynamic_index_in_dim(array, index, axis, keepdims=False)


def other_core(array):
    return shift(array, "c", NC, 1)


def reduce_tensor(parts):
    x, c = lax.axis_index("x"), lax.axis_index("c")
    parts = parts.reshape((NX, NC) + parts.shape[1:])
    received = other_core(take(parts, 1 - c, 1))
    chip = (take(parts, c, 1).astype(F32) + received.astype(F32)).astype(parts.dtype)
    near = [shift(take(chip, (x + d) % NX), "x", NX, d) for d in (1, -1)]
    far = take(chip, (x + 2) % NX)
    half = far.shape[0] // 2
    far = [shift(far[:half], "x", NX, 2), shift(far[half:], "x", NX, -2)]
    far = jnp.concatenate(far, axis=0)
    total = take(chip, x).astype(F32) + near[0].astype(F32)
    return total + near[1].astype(F32) + far.astype(F32)


def gather_tensor(block):
    x, c = lax.axis_index("x"), lax.axis_index("c")
    line = jnp.zeros((NX,) + block.shape, block.dtype)
    pieces = [(0, block)] + [(-d, shift(block, "x", NX, d)) for d in (1, -1, 2)]
    for step, piece in pieces:
        line = lax.dynamic_update_slice_in_dim(line, piece[None], (x + step) % NX, 0)
    other = other_core(line)
    low, high = jnp.where(c == 0, line, other), jnp.where(c == 0, other, line)
    return jnp.stack([low, high], axis=1)


def per_device(
    text_states,
    prompt_lengths,
    attn_gain,
    query_w,
    key_w,
    value_w,
    out_w,
    context_w,
    mod_scale,
    mod_shift,
    text_key_w,
    text_value_w,
    image_query,
    image_key,
    image_value,
):
    slots, enc = text_states.shape[1:]
    ndev = NX * NC
    pieces = NY * NZ
    me = lax.axis_index("x") * NC + lax.axis_index("c")
    width = query_w.shape[1]
    shard = query_w.shape[0]
    share = enc // ndev
    pad_rows = ((0, PADDED - PIECE), (0, 0))
    context_t = jnp.pad(context_w.T, pad_rows)
    text_w = jnp.pad(jnp.concatenate([text_key_w, text_value_w], axis=1), pad_rows)
    parts = [lane_blocks(w) for w in (query_w, key_w, context_t, text_w)]
    packed = jnp.concatenate(sum(parts, []), axis=0)
    context_row = 2 * width // 128 * shard
    text_row = context_row + share // 128 * PADDED
    out_rows = jnp.concatenate([out_w[:shard], out_w[shard:]], axis=1)
    second = jnp.concatenate([value_w, out_rows], axis=0)
    packed, second = lax.optimization_barrier((packed, second))
    gathered = lax.all_gather(packed, DP, axis=0)
    later = (text_states, image_query, image_key, image_value)
    ring, later = gather_weights(second, later)
    text_states, image_query, image_key, image_value = later

    flat = text_states[0].astype(F32)
    scale = lax.rsqrt(jnp.mean(flat * flat, axis=-1, keepdims=True) + EPS)
    normed = (flat * scale * attn_gain).astype(BF)

    nheads = image_query.shape[-1] // HEAD // ndev
    local = nheads * HEAD
    tokens = image_query.shape[1]
    image = jnp.concatenate(
        [
            jnp.swapaxes(part[0].reshape(tokens, ndev, local), 0, 1)
            for part in (image_query, image_key, image_value)
        ],
        axis=-1,
    )
    image = tensor_exchange(image).reshape(ndev * tokens, 3 * local)

    z = lax.axis_index("z")
    v_all = jnp.zeros((NY, NZ, shard, width), BF)
    w_out = jnp.zeros((NY, NZ, 2 * shard, shard), BF)
    for step, piece in ring:
        at = (z + step) % NZ
        v_all = lax.dynamic_update_slice_in_dim(v_all, piece[:, None, :shard], at, 1)
        rows = jnp.concatenate([piece[:, shard:, :128], piece[:, shard:, 128:]], axis=1)
        w_out = lax.dynamic_update_slice_in_dim(w_out, rows[:, None], at, 1)
    w_out = w_out.reshape(pieces, 2 * shard, shard)
    enc_v = jnp.dot(normed, v_all.reshape(enc, width), preferred_element_type=F32).astype(BF)

    def spaced(row):
        row = jnp.pad(row.reshape(pieces, PIECE), ((0, 0), (0, PADDED - PIECE)))
        return jnp.broadcast_to(row[:, :, None], (pieces, PADDED, 128))

    scale, move = spaced(mod_scale), spaced(mod_shift)
    mine = lax.dynamic_slice_in_dim(text_states[0], me * share, share, 1).astype(F32)
    mine = jnp.swapaxes(mine.reshape(slots, share // 128, 128), 0, 1)
    ready = lax.optimization_barrier((enc_v, image, w_out, scale, move, mine))
    enc_v, image, w_out, scale, move, mine = ready

    attn_part = encoder(prompt_lengths, normed, gathered, 0, enc_v, w_out)
    attn = reduce_tensor(attn_part.reshape(ndev, share // 128 * slots, 128))
    embedded = (mine + attn.reshape(mine.shape)).astype(BF)
    context_part = embed_context(embedded, gathered, context_row)
    context = reduce_tensor(context_part.reshape(ndev, pieces // ndev * PADDED, slots))
    context = gather_tensor(context.astype(BF)).reshape(pieces, PADDED, slots)
    result = joint(prompt_lengths, context, scale, move, image, gathered, text_row)
    result = tensor_exchange(result.reshape(ndev, tokens, local))
    return jnp.swapaxes(result, 0, 1).reshape(1, tokens, ndev * local)


def solution(mesh):
    fine = Mesh(mesh.devices.reshape(NY, NZ, NX, NC), DP + TENSOR)
    in_specs = (
        P(DP, None, None),
        P(DP),
        P(),
        P(DP, TENSOR),
        P(DP, TENSOR),
        P(DP, TENSOR),
        P(TENSOR, DP),
        P(TENSOR, DP),
        P(DP, None),
        P(DP, None),
        P(DP, TENSOR),
        P(DP, TENSOR),
        P(DP, TENSOR, None),
        P(DP, TENSOR, None),
        P(DP, TENSOR, None),
    )
    out_specs = P(DP, TENSOR, None)
    return jax.shard_map(
        per_device, mesh=fine, in_specs=in_specs, out_specs=out_specs, check_vma=False
    )
```

time: 262 us -> 227 us (0.87)
  waiting for transfers between devices: 135 us -> 85.3 us
  Pallas kernels: 0 us -> 19.6 us
  matrix products: 13.8 us -> 0.81 us
  local copies, waits for them, and re-layouts: 31.7 us -> 37.3 us
  other arithmetic: 7.4 us -> 10.7 us
    all_to_all x4 -> x1, waiting for transfers between devices: 61.9 us -> 0.01 us  [tensor_exchange(): return lax.all_to_all(array, TENSOR, 0, 0, tiled=True)]
    pallas_call x0 -> x3, Pallas kernels: none -> 19.6 us  [the longest x1 8.89 us: encoder(): pl.pallas_call(functools.partial(encoder_kernel, width // HEAD, steps), g...]
    ppermute x14 -> x26, starting transfers between devices: 21.2 us -> 40.6 us  [shift(): lax.ppermute(array, axis, [(i, (i + step) % size) for i in range(size)])]
    ppermute x14 -> x26, waiting for transfers between devices: 47.5 us -> 66.8 us  [shift(): lax.ppermute(array, axis, [(i, (i + step) % size) for i in range(size)])]
    all_to_all x2 -> x0, waiting for transfers between devices: 18.2 us -> none  [share_y(): lax.all_to_all(jnp.broadcast_to(block[None], (NY,) + block.shape), 'y', 0...]
    dot_general x9 -> x1, matrix products: 13.8 us -> 0.81 us  [per_device(): jnp.dot(normed, v_all.reshape(enc, width), preferred_element_type=F32)]
    all_to_all x4 -> x1, starting transfers between devices: 18.6 us -> 6.81 us  [tensor_exchange(): return lax.all_to_all(array, TENSOR, 0, 0, tiled=True)]
    unnamed x27 -> x43, local copies, waits for them, and re-layouts: 4.69 us -> 15.9 us
  transfers between devices with their start and end apart: 21 -> 28, of which waited for: 12 -> 17; matrix products, arithmetic and copies ran while one was open for 10% -> 11% of each run, Pallas kernels for 0% -> 0%
where the time goes in v2:
time: 227 us; the launch traced here: 226 us
  waiting for transfers between devices  85.3 us (38%)
  starting transfers between devices  47.5 us (21%)
  local copies, waits for them, and re-layouts  37.3 us (16%)
  Pallas kernels  19.6 us (9%)
  between operations  14.7 us (6%)
  other arithmetic  10.7 us (5%)
  blocking collectives  10 us (4%)
    ppermute x26, waiting for transfers between devices, shift(): lax.ppermute(array, axis, [(i, (i + step) % size) for i in range(size)])  66.8 us
    ppermute x26, starting transfers between devices, shift(): lax.ppermute(array, axis, [(i, (i + step) % size) for i in range(size)])  40.6 us
    all_gather x1, waiting for transfers between devices, per_device(): gathered = lax.all_gather(packed, DP, axis=0)  18.5 us
    unnamed x43, local copies, waits for them, and re-layouts  15.9 us
    all_to_all x1, blocking collectives, tensor_exchange(): return lax.all_to_all(array, TENSOR, 0, 0, tiled=True)  10 us
    pallas_call x1, Pallas kernels, encoder(): pl.pallas_call(functools.partial(encoder_kernel, width // HEAD, steps), g...  8.89 us
    pallas_call x1, Pallas kernels, joint(): pl.pallas_call(functools.partial(joint_kernel, row), in_specs=[pl.BlockSp...  7.22 us
    all_to_all x1, starting transfers between devices, tensor_exchange(): return lax.all_to_all(array, TENSOR, 0, 0, tiled=True)  6.81 us
  transfers between devices with their start and end apart: 28, of which 17 were waited for; matrix products, arithmetic and copies ran while one was open for 11% of the time, Pallas kernels for 0%

profile of v2, /device:TPU:1, one launch (start us, length us, event | category | flops | bytes accessed | tf_op | source)
XLA Modules:
  0.0 226.0 jit_solution(3334333018700678784)
XLA Ops:
  15.4 2.2 collective-permute-start
  23.8 2.7 %collective-permute-start.3 = (bf16[128,256]{1,0:T(8,128)(2,1)S(1)}, bf16[128,256]{1,0:T(8,128)(2,1)S(1)}, u32[]{:S(2)}, u32[]{:S(2)}) collective-permute-start(bf16[128,256]{1,0:T(8,128)(2,1)S(1)} %slice.200), channel_id=1, source_target_pairs={{0,192},{64,0},{128,64},{192,128},{1,193},{65,1},{129,65},{193,129... | collective-permute-start | bytes 196616 | tf_op jit(solution)/shard_map/ppermute | solution.py:24
  30.4 3.9 %collective-permute-start.5 = (bf16[4,256,256]{2,1,0:T(8,128)(2,1)}, bf16[4,256,256]{2,1,0:T(8,128)(2,1)}, u32[]{:S(2)}, u32[]{:S(2)}) collective-permute-start(bf16[4,256,256]{2,1,0:T(8,128)(2,1)} %fusion.37), channel_id=1, source_target_pairs={{0,56},{8,0},{16,8},{24,16},{32,24},{40,32},{48,40},{56,48},{1,57}... | collective-permute-start | bytes 1572872 | tf_op jit(solution)/shard_map/ppermute | solution.py:24
  36.3 6.8 %all-to-all-start = ((bf16[8,64,576]{2,1,0:T(8,128)(2,1)}), bf16[8,64,576]{2,1,0:T(8,128)(2,1)S(1)}, u32[]{:S(2)}, u32[]{:S(2)}) async-start(bf16[8,64,576]{2,1,0:T(8,128)(2,1)} %pad_maximum_fusion.1), calls=%async_computation | async-start | bytes 1310720 | tf_op jit(solution)/shard_map/all_to_all | solution.py:266
  43.1 2.5 %copy.48 = bf16[1,256,4096]{1,2,0:T(8,128)(2,1)} copy(bf16[1,256,4096]{2,1,0:T(8,128)(2,1)S(1)} %copy-done.7) | data formatting | bytes 4194304 | tf_op jit(solution)/shard_map/optimization_barrier | solution.py:40
  52.6 2.7 %collective-permute-start.7 = (bf16[4,256,256]{2,1,0:T(8,128)(2,1)}, bf16[4,256,256]{2,1,0:T(8,128)(2,1)S(1)}, u32[]{:S(2)}, u32[]{:S(2)}) collective-permute-start(bf16[4,256,256]{2,1,0:T(8,128)(2,1)} %collective-permute-done.5), channel_id=1, source_target_pairs={{0,56},{8,0},{16,8},{24,16},{32,24},{40,32},{48,40},{56,48},{1,57}... | collective-permute-start | bytes 1572872 | tf_op jit(solution)/shard_map/ppermute | solution.py:24
  59.3 9.2 %collective-permute-done.6 = bf16[4,256,256]{2,1,0:T(8,128)(2,1)S(1)} collective-permute-done((bf16[4,256,256]{2,1,0:T(8,128)(2,1)}, bf16[4,256,256]{2,1,0:T(8,128)(2,1)S(1)}, u32[]{:S(2)}, u32[]{:S(2)}) %collective-permute-start.6) | collective-permute-done | bytes 524320 | tf_op jit(solution)/shard_map/ppermute | solution.py:24
  68.9 2.3 %collective-permute-start.9 = (bf16[4,256,256]{2,1,0:T(8,128)(2,1)S(1)}, bf16[4,256,256]{2,1,0:T(8,128)(2,1)S(1)}, u32[]{:S(2)}, u32[]{:S(2)}) collective-permute-start(bf16[4,256,256]{2,1,0:T(8,128)(2,1)S(1)} %collective-permute-done.7), channel_id=1, source_target_pairs={{0,56},{8,0},{16,8},{24,16},{32,24},{40,32},{48,40},{56,48},{1,57}... | collective-permute-start | bytes 1572872 | tf_op jit(solution)/shard_map/ppermute | solution.py:24
  71.5 15.5 %collective-permute-done.8 = bf16[4,256,256]{2,1,0:T(8,128)(2,1)S(1)} collective-permute-done((bf16[4,256,256]{2,1,0:T(8,128)(2,1)S(1)}, bf16[4,256,256]{2,1,0:T(8,128)(2,1)S(1)}, u32[]{:S(2)}, u32[]{:S(2)}) %collective-permute-start.8) | collective-permute-done | bytes 524320 | tf_op jit(solution)/shard_map/ppermute | solution.py:24
  88.4 4.4 %collective-permute-done.9 = bf16[4,256,256]{2,1,0:T(8,128)(2,1)S(1)} collective-permute-done((bf16[4,256,256]{2,1,0:T(8,128)(2,1)S(1)}, bf16[4,256,256]{2,1,0:T(8,128)(2,1)S(1)}, u32[]{:S(2)}, u32[]{:S(2)}) %collective-permute-start.9) | collective-permute-done | bytes 524320 | tf_op jit(solution)/shard_map/ppermute | solution.py:24
  92.9 3.6 %collective-permute-start.11 = (bf16[2,256,256]{2,1,0:T(8,128)(2,1)S(1)}, bf16[2,256,256]{2,1,0:T(8,128)(2,1)S(1)}, u32[]{:S(2)}, u32[]{:S(2)}) collective-permute-start(bf16[2,256,256]{2,1,0:T(8,128)(2,1)S(1)} %slice.208), channel_id=1, source_target_pairs={{0,56},{8,0},{16,8},{24,16},{32,24},{40,32},{48,40},{56,48},{1,57}... | collective-permute-start | bytes 786440 | tf_op jit(solution)/shard_map/ppermute | solution.py:24
  96.8 4.0 %collective-permute-done.10 = bf16[2,256,256]{2,1,0:T(8,128)(2,1)S(1)} collective-permute-done((bf16[2,256,256]{2,1,0:T(8,128)(2,1)S(1)}, bf16[2,256,256]{2,1,0:T(8,128)(2,1)S(1)}, u32[]{:S(2)}, u32[]{:S(2)}) %collective-permute-start.10) | collective-permute-done | bytes 262176 | tf_op jit(solution)/shard_map/ppermute | solution.py:24
  100.8 6.2 %collective-permute-done.11 = bf16[2,256,256]{2,1,0:T(8,128)(2,1)S(1)} collective-permute-done((bf16[2,256,256]{2,1,0:T(8,128)(2,1)S(1)}, bf16[2,256,256]{2,1,0:T(8,128)(2,1)S(1)}, u32[]{:S(2)}, u32[]{:S(2)}) %collective-permute-start.11) | collective-permute-done | bytes 262176 | tf_op jit(solution)/shard_map/ppermute | solution.py:24
  110.6 2.2 broadcast_in_dim.123.shift_ref
  112.8 18.5 %all-gather.3.cloned.1.call-done = bf16[34304,128]{1,0:T(8,128)(2,1)} async-done(((bf16[1072,128]{1,0:T(8,128)(2,1)}), bf16[34304,128]{1,0:T(8,128)(2,1)}) %all-gather.3.cloned.1.call-update) | async-done | bytes 8781840 | tf_op jit(solution)/shard_map/all_gather | solution.py:336
  132.8 8.9 %shard_map.145 = bf16[32,256,128]{2,1,0:T(8,128)(2,1)S(1)} custom-call(s32[1]{0:T(128)S(6)} %copy.95.length_ref, bf16[256,4096]{1,0:T(8,128)(2,1)S(1)} %fusion.4.states_ref, bf16[32,1072,128]{2,1,0:T(8,128)(2,1)} %bitcast.192, bf16[256,256]{1,0:T(8,128)(2,1)S(1)} %fusion.14.v_ref, bf16[32,256,128]{2,1,0:T(8,128)(2,1)S(1)} %bitcast.197), custom_call_target="tpu_custom_call" | custom-call | flops 1610612736 | bytes 10485760 | tf_op jit(solution)/shard_map/pallas_call | solution.py:110
  143.7 2.3 %collective-permute-done.12 = bf16[4,1024,128]{2,1,0:T(8,128)(2,1)S(1)} collective-permute-done((bf16[4,1024,128]{2,1,0:T(8,128)(2,1)S(1)}, bf16[4,1024,128]{2,1,0:T(8,128)(2,1)S(1)}, u32[]{:S(2)}, u32[]{:S(2)}) %collective-permute-start.12) | collective-permute-done | bytes 1048608 | tf_op jit(solution)/shard_map/ppermute | solution.py:24
  154.0 6.2 %collective-permute-done.15 = bf16[512,128]{1,0:T(8,128)(2,1)S(1)} collective-permute-done((bf16[512,128]{1,0:T(8,128)(2,1)}, bf16[512,128]{1,0:T(8,128)(2,1)S(1)}, u32[]{:S(2)}, u32[]{:S(2)}) %collective-permute-start.15) | collective-permute-done | bytes 131104 | tf_op jit(solution)/shard_map/ppermute | solution.py:24
  160.2 2.9 %collective-permute-done.16 = bf16[512,128]{1,0:T(8,128)(2,1)} collective-permute-done((bf16[512,128]{1,0:T(8,128)(2,1)}, bf16[512,128]{1,0:T(8,128)(2,1)}, u32[]{:S(2)}, u32[]{:S(2)}) %collective-permute-start.16) | collective-permute-done | bytes 131104 | tf_op jit(solution)/shard_map/ppermute | solution.py:24
  164.4 3.5 %copy-done = bf16[34304,128]{1,0:T(8,128)(2,1)S(1)} copy-done((bf16[34304,128]{1,0:T(8,128)(2,1)S(1)}, bf16[34304,128]{1,0:T(8,128)(2,1)}, u32[]{:S(2)}) %copy-start) | copy-done | bytes 8781848
  167.8 3.5 %shard_map.146 = bf16[32,80,256]{2,1,0:T(8,128)(2,1)S(1)} custom-call(bf16[4,256,128]{2,1,0:T(8,128)(2,1)S(1)} %add_convert_fusion.embedded_ref, bf16[32,1072,128]{2,1,0:T(8,128)(2,1)S(1)} %bitcast.194), custom_call_target="tpu_custom_call" | custom-call | flops 671088640 | bytes 3932160 | tf_op jit(solution)/shard_map/pallas_call | solution.py:152
  172.7 1.9 collective-permute-done.17
  176.8 1.8 collective-permute-start.19
  178.9 2.8 %collective-permute-start.21 = (bf16[160,256]{1,0:T(8,128)(2,1)S(1)}, bf16[160,256]{1,0:T(8,128)(2,1)S(1)}, u32[]{:S(2)}, u32[]{:S(2)}) collective-permute-start(bf16[160,256]{1,0:T(8,128)(2,1)S(1)} %get-tuple-element.42), channel_id=1, source_target_pairs={{0,4},{2,6},{4,0},{6,2},{1,5},{3,7},{5,1},{7,3},{8,12},{10,14},{12... | collective-permute-start | bytes 245768 | tf_op jit(solution)/shard_map/ppermute | solution.py:24
  181.7 2.8 %collective-permute-done.20 = bf16[160,256]{1,0:T(8,128)(2,1)S(1)} collective-permute-done((bf16[160,256]{1,0:T(8,128)(2,1)S(1)}, bf16[160,256]{1,0:T(8,128)(2,1)S(1)}, u32[]{:S(2)}, u32[]{:S(2)}) %collective-permute-start.20) | collective-permute-done | bytes 81952 | tf_op jit(solution)/shard_map/ppermute | solution.py:24
  184.5 1.8 collective-permute-done.21
  187.0 2.1 collective-permute-start.23
  189.3 2.9 %collective-permute-done.22 = bf16[320,256]{1,0:T(8,128)(2,1)S(1)} collective-permute-done((bf16[320,256]{1,0:T(8,128)(2,1)S(1)}, bf16[320,256]{1,0:T(8,128)(2,1)S(1)}, u32[]{:S(2)}, u32[]{:S(2)}) %collective-permute-start.22) | collective-permute-done | bytes 163872 | tf_op jit(solution)/shard_map/ppermute | solution.py:24
  193.7 3.2 %collective-permute-done.24 = bf16[320,256]{1,0:T(8,128)(2,1)S(1)} collective-permute-done((bf16[320,256]{1,0:T(8,128)(2,1)S(1)}, bf16[320,256]{1,0:T(8,128)(2,1)S(1)}, u32[]{:S(2)}, u32[]{:S(2)}) %collective-permute-start.24) | collective-permute-done | bytes 163872 | tf_op jit(solution)/shard_map/ppermute | solution.py:24
  196.9 1.9 collective-permute-start.25
  200.8 7.2 %shard_map.147 = bf16[512,192]{1,0:T(8,128)(2,1)S(1)} custom-call(s32[1]{0:T(128)S(6)} %copy.95.length_ref, bf16[32,80,256]{2,1,0:T(8,128)(2,1)S(1)} %bitcast.200, f32[32,80,128]{2,1,0:T(8,128)S(1)} %broadcast_in_dim.122.scale_ref, f32[32,80,128]{2,1,0:T(8,128)S(1)} %copy-done.4, bf16[512,576]{1,0:T(8,128)(2,1)S(1)} %bitcast.201, ...), custom_call_target="tpu_custom_call" | custom-call | flops 805306368 | bytes 3276800 | tf_op jit(solution)/shard_map/pallas_call | solution.py:240
  208.0 10.0 %all_to_all.10 = bf16[8,64,192]{2,1,0:T(8,128)(2,1)S(1)} all-to-all(bf16[8,64,192]{2,1,0:T(8,128)(2,1)S(1)} %bitcast.202), channel_id=1, replica_groups=mesh['y'=4,'z'=8,'x'=4,'c'=2] {'x','c'}, dimensions={0} | all-to-all | bytes 393216 | tf_op jit(solution)/shard_map/all_to_all | solution.py:266
  (152 shorter events, 58.7 us)
Async XLA Ops:
  6.5 27.8 %copy-start.11 = (bf16[1,64,1536]{2,1,0:T(8,128)(2,1)S(1)}, bf16[1,64,1536]{2,1,0:T(8,128)(2,1)}, u32[]{:S(2)}) copy-start(bf16[1,64,1536]{2,1,0:T(8,128)(2,1)} %param.28) | copy-start | bytes 589828
  6.5 124.7 %all-gather.3.cloned.1.call-start = ((), (), s32[]{:S(2)}) async-start(), calls=%async_computation.2 | async-start | bytes 9056256 | tf_op jit(solution)/shard_map/all_gather | solution.py:336
  9.6 24.9 %copy-start.12 = (bf16[1,64,1536]{2,1,0:T(8,128)(2,1)S(1)}, bf16[1,64,1536]{2,1,0:T(8,128)(2,1)}, u32[]{:S(2)}) copy-start(bf16[1,64,1536]{2,1,0:T(8,128)(2,1)} %param.29) | copy-start | bytes 589828
  12.6 22.1 %copy-start.13 = (bf16[1,64,1536]{2,1,0:T(8,128)(2,1)S(1)}, bf16[1,64,1536]{2,1,0:T(8,128)(2,1)}, u32[]{:S(2)}) copy-start(bf16[1,64,1536]{2,1,0:T(8,128)(2,1)} %param.27) | copy-start | bytes 589828
  15.4 8.3 %collective-permute-start = (bf16[256,256]{1,0:T(8,128)(2,1)S(1)}, bf16[256,256]{1,0:T(8,128)(2,1)S(1)}, u32[]{:S(2)}, u32[]{:S(2)}) collective-permute-start(bf16[256,256]{1,0:T(8,128)(2,1)S(1)} %maximum_maximum_fusion), channel_id=1, source_target_pairs={{0,64},{64,128},{128,192},{192,0},{1,65},{65,129},{129,193},{193,1... | collective-permute-start | bytes 393224 | tf_op jit(solution)/shard_map/ppermute | solution.py:24
  17.6 6.2 %collective-permute-start.1 = (bf16[256,256]{1,0:T(8,128)(2,1)S(1)}, bf16[256,256]{1,0:T(8,128)(2,1)S(1)}, u32[]{:S(2)}, u32[]{:S(2)}) collective-permute-start(bf16[256,256]{1,0:T(8,128)(2,1)S(1)} %maximum_maximum_fusion), channel_id=1, source_target_pairs={{0,192},{64,0},{128,64},{192,128},{1,193},{65,1},{129,65},{193,129... | collective-permute-start | bytes 393224 | tf_op jit(solution)/shard_map/ppermute | solution.py:24
  23.6 4.4 %collective-permute-start.2 = (bf16[128,256]{1,0:T(8,128)(2,1)S(1)}, bf16[128,256]{1,0:T(8,128)(2,1)S(1)}, u32[]{:S(2)}, u32[]{:S(2)}) collective-permute-start(bf16[128,256]{1,0:T(8,128)(2,1)S(1)} %slice.199), channel_id=1, source_target_pairs={{0,64},{64,128},{128,192},{192,0},{1,65},{65,129},{129,193},{193,1... | collective-permute-start | bytes 196616 | tf_op jit(solution)/shard_map/ppermute | solution.py:24
  23.8 4.3 %collective-permute-start.3 = (bf16[128,256]{1,0:T(8,128)(2,1)S(1)}, bf16[128,256]{1,0:T(8,128)(2,1)S(1)}, u32[]{:S(2)}, u32[]{:S(2)}) collective-permute-start(bf16[128,256]{1,0:T(8,128)(2,1)S(1)} %slice.200), channel_id=1, source_target_pairs={{0,192},{64,0},{128,64},{192,128},{1,193},{65,1},{129,65},{193,129... | collective-permute-start | bytes 196616 | tf_op jit(solution)/shard_map/ppermute | solution.py:24
  28.7 23.8 %collective-permute-start.4 = (bf16[4,256,256]{2,1,0:T(8,128)(2,1)}, bf16[4,256,256]{2,1,0:T(8,128)(2,1)}, u32[]{:S(2)}, u32[]{:S(2)}) collective-permute-start(bf16[4,256,256]{2,1,0:T(8,128)(2,1)} %fusion.37), channel_id=1, source_target_pairs={{0,8},{8,16},{16,24},{24,32},{32,40},{40,48},{48,56},{56,0},{1,9},... | collective-permute-start | bytes 1572872 | tf_op jit(solution)/shard_map/ppermute | solution.py:24
  30.4 22.2 %collective-permute-start.5 = (bf16[4,256,256]{2,1,0:T(8,128)(2,1)}, bf16[4,256,256]{2,1,0:T(8,128)(2,1)}, u32[]{:S(2)}, u32[]{:S(2)}) collective-permute-start(bf16[4,256,256]{2,1,0:T(8,128)(2,1)} %fusion.37), channel_id=1, source_target_pairs={{0,56},{8,0},{16,8},{24,16},{32,24},{40,32},{48,40},{56,48},{1,57}... | collective-permute-start | bytes 1572872 | tf_op jit(solution)/shard_map/ppermute | solution.py:24
  36.3 73.1 %all-to-all-start = ((bf16[8,64,576]{2,1,0:T(8,128)(2,1)}), bf16[8,64,576]{2,1,0:T(8,128)(2,1)S(1)}, u32[]{:S(2)}, u32[]{:S(2)}) async-start(bf16[8,64,576]{2,1,0:T(8,128)(2,1)} %pad_maximum_fusion.1), calls=%async_computation | async-start | bytes 1310720 | tf_op jit(solution)/shard_map/all_to_all | solution.py:266
  52.5 16.1 %collective-permute-start.6 = (bf16[4,256,256]{2,1,0:T(8,128)(2,1)}, bf16[4,256,256]{2,1,0:T(8,128)(2,1)S(1)}, u32[]{:S(2)}, u32[]{:S(2)}) collective-permute-start(bf16[4,256,256]{2,1,0:T(8,128)(2,1)} %collective-permute-done.4), channel_id=1, source_target_pairs={{0,8},{8,16},{16,24},{24,32},{32,40},{40,48},{48,56},{56,0},{1,9},... | collective-permute-start | bytes 1572872 | tf_op jit(solution)/shard_map/ppermute | solution.py:24
  52.6 16.3 %collective-permute-start.7 = (bf16[4,256,256]{2,1,0:T(8,128)(2,1)}, bf16[4,256,256]{2,1,0:T(8,128)(2,1)S(1)}, u32[]{:S(2)}, u32[]{:S(2)}) collective-permute-start(bf16[4,256,256]{2,1,0:T(8,128)(2,1)} %collective-permute-done.5), channel_id=1, source_target_pairs={{0,56},{8,0},{16,8},{24,16},{32,24},{40,32},{48,40},{56,48},{1,57}... | collective-permute-start | bytes 1572872 | tf_op jit(solution)/shard_map/ppermute | solution.py:24
  68.6 18.5 %collective-permute-start.8 = (bf16[4,256,256]{2,1,0:T(8,128)(2,1)S(1)}, bf16[4,256,256]{2,1,0:T(8,128)(2,1)S(1)}, u32[]{:S(2)}, u32[]{:S(2)}) collective-permute-start(bf16[4,256,256]{2,1,0:T(8,128)(2,1)S(1)} %collective-permute-done.6), channel_id=1, source_target_pairs={{0,8},{8,16},{16,24},{24,32},{32,40},{40,48},{48,56},{56,0},{1,9},... | collective-permute-start | bytes 1572872 | tf_op jit(solution)/shard_map/ppermute | solution.py:24
  68.9 23.9 %collective-permute-start.9 = (bf16[4,256,256]{2,1,0:T(8,128)(2,1)S(1)}, bf16[4,256,256]{2,1,0:T(8,128)(2,1)S(1)}, u32[]{:S(2)}, u32[]{:S(2)}) collective-permute-start(bf16[4,256,256]{2,1,0:T(8,128)(2,1)S(1)} %collective-permute-done.7), channel_id=1, source_target_pairs={{0,56},{8,0},{16,8},{24,16},{32,24},{40,32},{48,40},{56,48},{1,57}... | collective-permute-start | bytes 1572872 | tf_op jit(solution)/shard_map/ppermute | solution.py:24
  87.1 13.7 %collective-permute-start.10 = (bf16[2,256,256]{2,1,0:T(8,128)(2,1)S(1)}, bf16[2,256,256]{2,1,0:T(8,128)(2,1)S(1)}, u32[]{:S(2)}, u32[]{:S(2)}) collective-permute-start(bf16[2,256,256]{2,1,0:T(8,128)(2,1)S(1)} %slice.207), channel_id=1, source_target_pairs={{0,8},{8,16},{16,24},{24,32},{32,40},{40,48},{48,56},{56,0},{1,9},... | collective-permute-start | bytes 786440 | tf_op jit(solution)/shard_map/ppermute | solution.py:24
  92.9 14.1 %collective-permute-start.11 = (bf16[2,256,256]{2,1,0:T(8,128)(2,1)S(1)}, bf16[2,256,256]{2,1,0:T(8,128)(2,1)S(1)}, u32[]{:S(2)}, u32[]{:S(2)}) collective-permute-start(bf16[2,256,256]{2,1,0:T(8,128)(2,1)S(1)} %slice.208), channel_id=1, source_target_pairs={{0,56},{8,0},{16,8},{24,16},{32,24},{40,32},{48,40},{56,48},{1,57}... | collective-permute-start | bytes 786440 | tf_op jit(solution)/shard_map/ppermute | solution.py:24
  143.2 2.8 %collective-permute-start.12 = (bf16[4,1024,128]{2,1,0:T(8,128)(2,1)S(1)}, bf16[4,1024,128]{2,1,0:T(8,128)(2,1)S(1)}, u32[]{:S(2)}, u32[]{:S(2)}) collective-permute-start(bf16[4,1024,128]{2,1,0:T(8,128)(2,1)S(1)} %dynamic-slice_bitcast_fusion), channel_id=1, source_target_pairs={{0,1},{1,0},{2,3},{3,2},{4,5},{5,4},{6,7},{7,6},{8,9},{9,8},{10,11... | collective-permute-start | bytes 3145736 | tf_op jit(solution)/shard_map/ppermute | solution.py:24
  147.5 16.8 %copy-start.9 = (f32[256,4,128]{2,0,1:T(8,128)S(1)}, f32[256,4,128]{2,0,1:T(8,128)}, u32[]{:S(2)}) copy-start(f32[256,4,128]{2,0,1:T(8,128)} %copy.49) | copy-start | bytes 1572868
  147.6 15.5 %collective-permute-start.13 = (bf16[1024,128]{1,0:T(8,128)(2,1)S(1)}, bf16[1024,128]{1,0:T(8,128)(2,1)}, u32[]{:S(2)}, u32[]{:S(2)}) collective-permute-start(bf16[1024,128]{1,0:T(8,128)(2,1)S(1)} %get-tuple-element.37), channel_id=1, source_target_pairs={{0,2},{2,4},{4,6},{6,0},{1,3},{3,5},{5,7},{7,1},{8,10},{10,12},{12... | collective-permute-start | bytes 786440 | tf_op jit(solution)/shard_map/ppermute | solution.py:24
  148.9 14.2 %collective-permute-start.14 = (bf16[1024,128]{1,0:T(8,128)(2,1)S(1)}, bf16[1024,128]{1,0:T(8,128)(2,1)}, u32[]{:S(2)}, u32[]{:S(2)}) collective-permute-start(bf16[1024,128]{1,0:T(8,128)(2,1)S(1)} %get-tuple-element.38), channel_id=1, source_target_pairs={{0,6},{2,0},{4,2},{6,4},{1,7},{3,1},{5,3},{7,5},{8,14},{10,8},{12,... | collective-permute-start | bytes 786440 | tf_op jit(solution)/shard_map/ppermute | solution.py:24
  151.0 9.1 %collective-permute-start.15 = (bf16[512,128]{1,0:T(8,128)(2,1)}, bf16[512,128]{1,0:T(8,128)(2,1)S(1)}, u32[]{:S(2)}, u32[]{:S(2)}) collective-permute-start(bf16[512,128]{1,0:T(8,128)(2,1)} %get-tuple-element.35), channel_id=1, source_target_pairs={{0,4},{2,6},{4,0},{6,2},{1,5},{3,7},{5,1},{7,3},{8,12},{10,14},{12... | collective-permute-start | bytes 393224 | tf_op jit(solution)/shard_map/ppermute | solution.py:24
  152.5 10.5 %collective-permute-start.16 = (bf16[512,128]{1,0:T(8,128)(2,1)}, bf16[512,128]{1,0:T(8,128)(2,1)}, u32[]{:S(2)}, u32[]{:S(2)}) collective-permute-start(bf16[512,128]{1,0:T(8,128)(2,1)} %get-tuple-element.36), channel_id=1, source_target_pairs={{0,4},{2,6},{4,0},{6,2},{1,5},{3,7},{5,1},{7,3},{8,12},{10,14},{12... | collective-permute-start | bytes 393224 | tf_op jit(solution)/shard_map/ppermute | solution.py:24
  171.4 3.1 %collective-permute-start.17 = (bf16[4,320,256]{2,1,0:T(8,128)(2,1)S(1)}, bf16[4,320,256]{2,1,0:T(8,128)(2,1)}, u32[]{:S(2)}, u32[]{:S(2)}) collective-permute-start(bf16[4,320,256]{2,1,0:T(8,128)(2,1)S(1)} %dynamic-slice_bitcast_fusion.1), channel_id=1, source_target_pairs={{0,1},{1,0},{2,3},{3,2},{4,5},{5,4},{6,7},{7,6},{8,9},{9,8},{10,11... | collective-permute-start | bytes 1966088 | tf_op jit(solution)/shard_map/ppermute | solution.py:24
  175.9 10.4 %collective-permute-start.18 = (bf16[320,256]{1,0:T(8,128)(2,1)S(1)}, bf16[320,256]{1,0:T(8,128)(2,1)S(1)}, u32[]{:S(2)}, u32[]{:S(2)}) collective-permute-start(bf16[320,256]{1,0:T(8,128)(2,1)S(1)} %get-tuple-element.39), channel_id=1, source_target_pairs={{0,2},{2,4},{4,6},{6,0},{1,3},{3,5},{5,7},{7,1},{8,10},{10,12},{12... | collective-permute-start | bytes 491528 | tf_op jit(solution)/shard_map/ppermute | solution.py:24
  176.8 9.5 %collective-permute-start.19 = (bf16[320,256]{1,0:T(8,128)(2,1)S(1)}, bf16[320,256]{1,0:T(8,128)(2,1)S(1)}, u32[]{:S(2)}, u32[]{:S(2)}) collective-permute-start(bf16[320,256]{1,0:T(8,128)(2,1)S(1)} %get-tuple-element.40), channel_id=1, source_target_pairs={{0,6},{2,0},{4,2},{6,4},{1,7},{3,1},{5,3},{7,5},{8,14},{10,8},{12,... | collective-permute-start | bytes 491528 | tf_op jit(solution)/shard_map/ppermute | solution.py:24
  178.6 5.9 %collective-permute-start.20 = (bf16[160,256]{1,0:T(8,128)(2,1)S(1)}, bf16[160,256]{1,0:T(8,128)(2,1)S(1)}, u32[]{:S(2)}, u32[]{:S(2)}) collective-permute-start(bf16[160,256]{1,0:T(8,128)(2,1)S(1)} %get-tuple-element.41), channel_id=1, source_target_pairs={{0,4},{2,6},{4,0},{6,2},{1,5},{3,7},{5,1},{7,3},{8,12},{10,14},{12... | collective-permute-start | bytes 245768 | tf_op jit(solution)/shard_map/ppermute | solution.py:24
  178.9 7.3 %collective-permute-start.21 = (bf16[160,256]{1,0:T(8,128)(2,1)S(1)}, bf16[160,256]{1,0:T(8,128)(2,1)S(1)}, u32[]{:S(2)}, u32[]{:S(2)}) collective-permute-start(bf16[160,256]{1,0:T(8,128)(2,1)S(1)} %get-tuple-element.42), channel_id=1, source_target_pairs={{0,4},{2,6},{4,0},{6,2},{1,5},{3,7},{5,1},{7,3},{8,12},{10,14},{12... | collective-permute-start | bytes 245768 | tf_op jit(solution)/shard_map/ppermute | solution.py:24
  186.4 5.8 %collective-permute-start.22 = (bf16[320,256]{1,0:T(8,128)(2,1)S(1)}, bf16[320,256]{1,0:T(8,128)(2,1)S(1)}, u32[]{:S(2)}, u32[]{:S(2)}) collective-permute-start(bf16[320,256]{1,0:T(8,128)(2,1)S(1)} %get-tuple-element.32), channel_id=1, source_target_pairs={{0,2},{2,4},{4,6},{6,0},{1,3},{3,5},{5,7},{7,1},{8,10},{10,12},{12... | collective-permute-start | bytes 491528 | tf_op jit(solution)/shard_map/ppermute | solution.py:24
  187.0 6.6 %collective-permute-start.23 = (bf16[320,256]{1,0:T(8,128)(2,1)S(1)}, bf16[320,256]{1,0:T(8,128)(2,1)S(1)}, u32[]{:S(2)}, u32[]{:S(2)}) collective-permute-start(bf16[320,256]{1,0:T(8,128)(2,1)S(1)} %get-tuple-element.32), channel_id=1, source_target_pairs={{0,6},{2,0},{4,2},{6,4},{1,7},{3,1},{5,3},{7,5},{8,14},{10,8},{12,... | collective-permute-start | bytes 491528 | tf_op jit(solution)/shard_map/ppermute | solution.py:24
  189.2 7.7 %collective-permute-start.24 = (bf16[320,256]{1,0:T(8,128)(2,1)S(1)}, bf16[320,256]{1,0:T(8,128)(2,1)S(1)}, u32[]{:S(2)}, u32[]{:S(2)}) collective-permute-start(bf16[320,256]{1,0:T(8,128)(2,1)S(1)} %get-tuple-element.32), channel_id=1, source_target_pairs={{0,4},{2,6},{4,0},{6,2},{1,5},{3,7},{5,1},{7,3},{8,12},{10,14},{12... | collective-permute-start | bytes 491528 | tf_op jit(solution)/shard_map/ppermute | solution.py:24
  196.9 3.6 %collective-permute-start.25 = (bf16[4,320,256]{2,1,0:T(8,128)(2,1)S(1)}, bf16[4,320,256]{2,1,0:T(8,128)(2,1)S(1)}, u32[]{:S(2)}, u32[]{:S(2)}) collective-permute-start(bf16[4,320,256]{2,1,0:T(8,128)(2,1)S(1)} %bitcast_dynamic-update-slice_fusion.1), channel_id=1, source_target_pairs={{0,1},{1,0},{2,3},{3,2},{4,5},{5,4},{6,7},{7,6},{8,9},{9,8},{10,11... | collective-permute-start | bytes 1966088 | tf_op jit(solution)/shard_map/ppermute | solution.py:24
  (12 other events, 38.3 us)
Sparse Core Ops, SparseCore 0:
  15.5 115.7 all-gather.2
